TPU v7x, 512 devices: a whole 4x4x16 slice. The times are simulated.
512 devices in a mesh: seq: 64 (over z, y), head: 8 (over x, core).
Axes of the slice: x: 4, y: 4, z: 16, core: 2. Of those that a mesh axis runs over, the one named last changes fastest.
Arguments:
- queries: bfloat16 [16384, 4096], P('seq', 'head'), may hold values from -1.796875 to 1.796875
- key_rows: bfloat16 [16384, 4096], P('seq', 'head'), may hold values from -1.796875 to 1.796875
- values: bfloat16 [16384, 4096], P('seq', 'head'), may hold values from -100 to 100
- out_weight: bfloat16 [4096, 4096], P('head', 'seq'), may hold values from -0.25 to 0.25
- out_grad: bfloat16 [16384, 4096], P('seq', 'head'), may hold values from -6 to 6
Outputs:
- mixed: bfloat16 [16384, 4096], P('seq', 'head')
- query_grad: bfloat16 [16384, 4096], P('seq', 'head')
- key_grad: bfloat16 [16384, 4096], P('seq', 'head')
- value_grad: bfloat16 [16384, 4096], P('seq', 'head')
All inputs are finite; a program needn't handle non-finite values.
Results may differ from a plain program's by a relative error of at most 0.014.
Values may be sent and summed in bfloat16 or wider, within the bound.
No kernel may reach another device: no remote copies, remote signals or barrier semaphores. Data moves between devices by JAX's collectives and lax.ppermute only.
A program may use at most 64 MiB of HBM per device.

v0:
```python
import jax
import jax.numpy as jnp
from jax import lax
from jax.sharding import PartitionSpec as P

HEAD_DIM = 128


def prefix_2(value, axis, combine, identity):
    length, position = (lax.axis_size(axis), lax.axis_index(axis))
    everything = lax.all_gather(value, axis)
    start = jnp.broadcast_to(jnp.asarray(identity, value.dtype), value.shape)

    def hop(k, before):
        reached = k < position
        new = combine(before, everything[k])
        return jnp.where(reached, new, before)

    return lax.fori_loop(0, length, hop, start)


def prefix_3(value, axis, combine, identity):
    length, position = (lax.axis_size(axis), lax.axis_index(axis))
    everything = lax.all_gather(value.astype(jnp.bfloat16), axis)
    start = jnp.broadcast_to(jnp.asarray(identity, value.dtype), value.shape)

    def hop(k, before):
        at = length - 1 - k
        reached = at > position
        new = combine(before, everything[at].astype(value.dtype))
        return jnp.where(reached, new, before)

    return lax.fori_loop(0, length, hop, start)


def lower_mask(length):
    row_ids = lax.broadcasted_iota(jnp.int32, (length, length), 0)
    col_ids = lax.broadcasted_iota(jnp.int32, (length, length), 1)
    return row_ids >= col_ids


def add_states(earlier, latter):
    return earlier + latter


def contract_cols(left_side, right_side):
    return lax.dot_general(
        left_side, right_side, (((1,), (1,)), ((), ())), preferred_element_type=jnp.float32
    )


def per_device(queries, key_rows, values, out_weight, out_grad):
    length = queries.shape[0]
    heads_here = queries.shape[1] // HEAD_DIM
    query_heads = queries.reshape(length, heads_here, HEAD_DIM)
    key_heads = key_rows.reshape(length, heads_here, HEAD_DIM)
    value_heads = values.reshape(length, heads_here, HEAD_DIM)
    causal = lower_mask(length)[None]
    local_state = jnp.einsum(
        "shd,she->hde", key_heads, value_heads, preferred_element_type=jnp.float32
    )
    prefix = prefix_2(local_state, "seq", add_states, jnp.zeros_like(local_state))
    prefix_low = prefix.astype(jnp.bfloat16)
    scores = jnp.einsum("thd,shd->hts", query_heads, key_heads, preferred_element_type=jnp.float32)
    weights = jnp.where(causal, scores, 0.0).astype(jnp.bfloat16)
    numerator = jnp.einsum("hts,she->the", weights, value_heads, preferred_element_type=jnp.float32)
    numerator = numerator + jnp.einsum(
        "thd,hde->the", query_heads, prefix_low, preferred_element_type=jnp.float32
    )
    spread = jnp.sqrt(jnp.mean(numerator * numerator, axis=-1, keepdims=True) + 1e-06)
    normed = numerator / spread
    attended = normed.astype(jnp.bfloat16).reshape(length, heads_here * HEAD_DIM)
    full_weight = lax.all_gather(out_weight, "seq", axis=1, tiled=True)
    partial_value = jnp.dot(attended, full_weight, preferred_element_type=jnp.float32)
    layer_out = lax.psum_scatter(
        partial_value.astype(jnp.bfloat16), "head", scatter_dimension=1, tiled=True
    )
    out_dir = contract_cols(lax.all_gather(out_grad, "head", axis=1, tiled=True), full_weight)
    out_dir = out_dir.reshape(length, heads_here, HEAD_DIM)
    along_dir = jnp.mean(out_dir * normed, axis=-1, keepdims=True)
    numer_grad = ((out_dir - normed * along_dir) / spread).astype(jnp.bfloat16)
    local_grad = jnp.einsum(
        "thd,the->hde", query_heads, numer_grad, preferred_element_type=jnp.float32
    )
    suffix = prefix_3(local_grad, "seq", add_states, jnp.zeros_like(local_grad))
    suffix_low = suffix.astype(jnp.bfloat16)
    pair_scores = jnp.einsum(
        "the,she->hts", numer_grad, value_heads, preferred_element_type=jnp.float32
    )
    pair_low = jnp.where(causal, pair_scores, 0.0).astype(jnp.bfloat16)
    query_out = jnp.einsum("hts,shd->thd", pair_low, key_heads, preferred_element_type=jnp.float32)
    query_out = query_out + jnp.einsum(
        "the,hde->thd", numer_grad, prefix_low, preferred_element_type=jnp.float32
    )
    key_out = jnp.einsum("hts,thd->shd", pair_low, query_heads, preferred_element_type=jnp.float32)
    key_out = key_out + jnp.einsum(
        "she,hde->shd", value_heads, suffix_low, preferred_element_type=jnp.float32
    )
    value_out = jnp.einsum("hts,the->she", weights, numer_grad, preferred_element_type=jnp.float32)
    value_out = value_out + jnp.einsum(
        "shd,hde->she", key_heads, suffix_low, preferred_element_type=jnp.float32
    )
    flat_shape = (length, heads_here * HEAD_DIM)
    return (
        layer_out,
        query_out.reshape(flat_shape).astype(jnp.bfloat16),
        key_out.reshape(flat_shape).astype(jnp.bfloat16),
        value_out.reshape(flat_shape).astype(jnp.bfloat16),
    )


def solution(mesh):
    placed = (
        P("seq", "head"),
        P("seq", "head"),
        P("seq", "head"),
        P("head", "seq"),
        P("seq", "head"),
    )
    return jax.shard_map(
        per_device,
        mesh=mesh,
        in_specs=placed,
        out_specs=(P("seq", "head"), P("seq", "head"), P("seq", "head"), P("seq", "head")),
        check_vma=False,
    )
```

profile of v0, /device:TPU:2, one launch (start us, length us, event | category | flops | bytes accessed | tf_op | source)
XLA Modules:
  0.0 625.4 jit_solution(14009342310516333591)
XLA Ops:
  7.2 1.1 copy.99
  8.3 1.9 fusion.12
  11.8 1.2 fusion
  13.1 1.3 convolution_bitcast_fusion.5
  14.4 195.2 %all-gather.11.cloned.1.call-done = f32[256,128,128]{2,1,0:T(8,128)} async-done(((f32[4,128,128]{2,1,0:T(8,128)}), f32[256,128,128]{2,1,0:T(8,128)}) %all-gather.11.cloned.1.call-update) | async-done | bytes 16777232 | tf_op jit(solution)/shard_map/all_gather | solution.py:11
  209.5 68.2 %while.30 = (s32[]{:T(128)}, f32[4,128,128]{2,1,0:T(8,128)S(1)}, s32[]{:T(128)}, f32[64,4,128,128]{3,2,1,0:T(8,128)}, s32[]{:T(128)}, /*index=5*/s32[]{:T(128)}) while((s32[]{:T(128)}, f32[4,128,128]{2,1,0:T(8,128)S(1)}, s32[]{:T(128)}, f32[64,4,128,128]{3,2,1,0:T(8,128)}, s32[]{:T(128)}, /*index=5*/s32[]{:T(128)}) %tuple.93), condition=%wide.region_1.2_spmd.clone, body=%wide.region_0.1_spmd.clone.sunk | while | flops 196612 | bytes 786525 | solution.py:19
  210.6 1.0 add_select_fusion.4
  211.6 1.0 add_select_fusion.4
  212.7 1.0 add_select_fusion.4
  213.8 1.0 add_select_fusion.4
  214.8 1.0 add_select_fusion.4
  215.9 1.0 add_select_fusion.4
  223.4 1.0 add_select_fusion.4
  224.4 1.1 add_select_fusion.4
  225.5 1.1 add_select_fusion.4
  227.7 1.0 add_select_fusion.4
  229.8 1.0 add_select_fusion.4
  230.9 1.0 add_select_fusion.4
  231.9 1.0 add_select_fusion.4
  234.1 1.0 add_select_fusion.4
  235.1 1.0 add_select_fusion.4
  237.3 1.0 add_select_fusion.4
  239.4 1.0 add_select_fusion.4
  249.0 1.0 add_select_fusion.4
  251.1 1.0 add_select_fusion.4
  253.2 1.0 add_select_fusion.4
  255.4 1.0 add_select_fusion.4
  257.5 1.0 add_select_fusion.4
  259.6 1.0 add_select_fusion.4
  269.2 1.0 add_select_fusion.4
  271.3 1.0 add_select_fusion.4
  272.4 1.0 add_select_fusion.4
  274.5 1.0 add_select_fusion.4
  276.7 1.0 add_select_fusion.4
  278.0 112.8 %all-gather.7.cloned.1.call-done = bf16[512,4096]{0,1:T(8,128)(2,1)} async-done(((bf16[512,64]{0,1:T(8,128)(2,1)}), bf16[512,4096]{0,1:T(8,128)(2,1)}) %all-gather.7.cloned.1.call-update) | async-done | bytes 4194320 | tf_op jit(solution)/shard_map/all_gather | solution.py:73
  390.9 4.6 multiply_reduce_fusion
  398.9 4.9 convolution_convert_fusion
  403.8 144.5 %all-gather.13.cloned.1.call-done = bf16[256,128,128]{2,1,0:T(8,128)(2,1)} async-done(((bf16[4,128,128]{2,1,0:T(8,128)(2,1)}), bf16[256,128,128]{2,1,0:T(8,128)(2,1)}) %all-gather.13.cloned.1.call-update) | async-done | bytes 8388624 | tf_op jit(solution)/shard_map/all_gather | solution.py:24
  548.4 68.3 %while.31 = (s32[]{:T(128)}, f32[4,128,128]{2,1,0:T(8,128)S(1)}, s32[]{:T(128)}, bf16[64,4,128,128]{3,2,1,0:T(8,128)(2,1)}, s32[]{:T(128)}, /*index=5*/s32[]{:T(128)}, s32[]{:T(128)}, s32[]{:T(128)}) while((s32[]{:T(128)}, f32[4,128,128]{2,1,0:T(8,128)S(1)}, s32[]{:T(128)}, bf16[64,4,128,128]{3,2,1,0:T(8,128)(2,1)}, s32[]{:T(128)}, ...), condition=%wide.region_6.7_spmd.clone, body=%wide.region_5.6_spmd.clone.sunk | while | flops 262152 | bytes 655515 | solution.py:33
  562.2 1.1 add_select_fusion.5
  564.4 1.0 add_select_fusion.5
  568.7 1.0 add_select_fusion.5
  570.8 1.0 add_select_fusion.5
  574.0 1.0 add_select_fusion.5
  577.2 1.0 add_select_fusion.5
  580.4 1.0 add_select_fusion.5
  582.6 1.0 add_select_fusion.5
  583.6 1.0 add_select_fusion.5
  (128 shorter events, 102.0 us)
Async XLA Ops:
  7.2 4.7 copy-start
  7.2 202.3 %all-gather.11.cloned.1.call-start = ((), (), s32[]{:S(2)}) async-start(), calls=%async_computation.4 | async-start | bytes 17039360 | tf_op jit(solution)/shard_map/all_gather | solution.py:11
  10.2 267.8 %all-gather.9.cloned.1.call-start = ((), (), s32[]{:S(2)}) async-start(), calls=%async_computation.3 | async-start | bytes 2359296 | tf_op jit(solution)/shard_map/all_gather | solution.py:78
  11.0 379.9 %all-gather.7.cloned.1.call-start = ((), (), s32[]{:S(2)}) async-start(), calls=%async_computation.1 | async-start | bytes 4259840 | tf_op jit(solution)/shard_map/all_gather | solution.py:73
  11.7 536.6 %all-gather.13.cloned.1.call-start = ((), (), s32[]{:S(2)}) async-start(), calls=%async_computation.5 | async-start | bytes 8519680 | tf_op jit(solution)/shard_map/all_gather | solution.py:24
  390.9 5.8 copy-start.1
  396.6 222.3 %reduce-scatter.2.cloned.1.call-start = ((), (), s32[]{:S(2)}) async-start(), calls=%async_computation.2 | async-start | bytes 2359296 | tf_op jit(solution)/shard_map/reduce_scatter | solution.py:75
  403.8 212.9 %copy-start.2 = (bf16[256,512]{1,0:T(8,128)(2,1)S(1)}, bf16[256,512]{1,0:T(8,128)(2,1)}, u32[]{:S(2)}) copy-start(bf16[256,512]{1,0:T(8,128)(2,1)} %param.10) | copy-start | bytes 786436
Sparse Core Ops, SparseCore 0:
  11.5 197.9 all-gather.10
  211.6 28.2 all-gather.8
  242.9 147.8 all-gather.6
  396.7 151.5 all-gather.12
  551.6 32.7 reduce-scatter.1
where the time goes:
time: 629 us; the launch traced here: 625 us
  waiting for transfers between devices  454 us (72%)
  other arithmetic  133 us (21%)
  matrix products  16.2 us (3%)
  between operations  14 us (2%)
    all_gather x1, waiting for transfers between devices, prefix_2(): everything = lax.all_gather(value, axis)  195 us
    all_gather x1, waiting for transfers between devices, prefix_3(): everything = lax.all_gather(value.astype(jnp.bfloat16), axis)  145 us
    select_n x128, other arithmetic, hop(): return jnp.where(reached, new, before)  133 us
    all_gather x1, waiting for transfers between devices, per_device(): full_weight = lax.all_gather(out_weight, 'seq', axis=1, tiled=True)  113 us
  transfers between devices with their start and end apart: 5, of which 3 were waited for; matrix products, arithmetic and copies ran while one was open for 23% of the time, Pallas kernels for 0%

commit v1 on v0

v1 whole, which is shorter than its diff:
```python
import jax
import jax.numpy as jnp
from jax import lax
from jax.experimental import pallas as pl
from jax.experimental.pallas import tpu as pltpu
from jax.sharding import Mesh, PartitionSpec as P

HEAD_DIM = 128
NEAR = 16
F32 = jnp.float32
BF16 = jnp.bfloat16
AXES = ("zh", "zl", "y", "x", "core")
SIZES = (4, 4, 4, 4, 2)
PARAMS = pltpu.CompilerParams(vmem_limit_bytes=40 * 1024 * 1024)


def dot(left, right, dims):
    return lax.dot_general(left, right, (dims, ((), ())), preferred_element_type=F32)


def shape_of(dims, dtype):
    return jax.ShapeDtypeStruct(dims, dtype)


def call(kernel, out_shape, *operands, smem=0, after=(), name=None):
    count = len(operands)
    spaces = [pltpu.SMEM] * smem + [pltpu.VMEM] * (count - smem) + [pl.ANY] * len(after)
    operands = operands + tuple(after)

    def body(*refs):
        kernel(*refs[:count], *refs[count + len(after) :])

    return pl.pallas_call(
        body,
        out_shape=out_shape,
        in_specs=[pl.BlockSpec(memory_space=s) for s in spaces],
        compiler_params=PARAMS,
        name=name,
    )(*operands)


def head_cols(head):
    return slice(head * HEAD_DIM, (head + 1) * HEAD_DIM)


def causal_mask(length):
    rows = lax.broadcasted_iota(jnp.int32, (length, length), 0)
    cols = lax.broadcasted_iota(jnp.int32, (length, length), 1)
    return rows >= cols


def state_kernel(left_ref, right_ref, out_ref):
    for head in range(left_ref.shape[1] // HEAD_DIM):
        cols = head_cols(head)
        out_ref[cols, :] = dot(left_ref[:, cols], right_ref[:, cols], ((0,), (0,))).astype(BF16)


def near_kernel(reverse, pieces_ref, *refs):
    scan_ref, total_ref = refs[-3:-1] if len(refs) > 2 else refs
    for at, grad_ref in enumerate(refs[:-3]):
        refs[-1][at] = grad_ref[...]
    count = pieces_ref.shape[0]
    running = jnp.zeros(pieces_ref.shape[1:], F32)
    for step in range(count):
        at = count - 1 - step if reverse else step
        scan_ref[at] = running
        running = running + pieces_ref[at].astype(F32)
    total = running.astype(BF16)
    for at in range(total_ref.shape[0]):
        total_ref[at] = total


def far_kernel(reverse, group_ref, scan_ref, totals_ref, out_ref):
    group = group_ref[0]
    offset = jnp.zeros(scan_ref.shape[1:], F32)
    for other in range(totals_ref.shape[0]):
        counts = other > group if reverse else other < group
        offset = offset + jnp.where(counts, totals_ref[other].astype(F32), 0.0)
    for at in range(scan_ref.shape[0]):
        out_ref[at] = (scan_ref[at] + offset).astype(BF16)


def outside_sum(local, group, reverse, grads=()):
    near = ("zl", "y")
    piece = (NEAR, local.shape[0] // NEAR, HEAD_DIM)
    pieces = lax.all_to_all(local.reshape(piece), near, 0, 0, tiled=True)
    stacked = (shape_of((len(grads),) + grads[0].shape, BF16),) if grads else ()
    scan, total, *stack = call(
        lambda *refs: near_kernel(reverse, *refs),
        (shape_of(piece, F32), shape_of((SIZES[0],) + piece[1:], BF16)) + stacked,
        pieces, *grads,
        name="near_scan",
    )
    stack += [permute(own, lambda across, half: (across, 1 - half)) for own in stack]
    totals = lax.all_to_all(total, "zh", 0, 0, tiled=True)
    sums = call(
        lambda *refs: far_kernel(reverse, *refs),
        shape_of(piece, BF16),
        group,
        scan,
        totals,
        smem=1,
        after=stack,
        name="far_scan",
    )
    return lax.all_to_all(sums, near, 0, 0, tiled=True).reshape(local.shape), *stack


def forward_kernel(query_ref, key_ref, value_ref, prefix_ref, numer_ref, attended_ref):
    causal = causal_mask(query_ref.shape[0])
    for head in range(query_ref.shape[1] // HEAD_DIM):
        cols = head_cols(head)
        query = query_ref[:, cols]
        scores = dot(query, key_ref[:, cols], ((1,), (1,)))
        weights = jnp.where(causal, scores, 0.0).astype(BF16)
        numer = dot(weights, value_ref[:, cols], ((1,), (0,)))
        numer = numer + dot(query, prefix_ref[cols, :], ((1,), (0,)))
        spread = jnp.sqrt(jnp.mean(numer * numer, axis=-1, keepdims=True) + 1e-06)
        numer_ref[:, cols] = numer
        attended_ref[:, cols] = (numer / spread).astype(BF16)


def middle_kernel(
    place_ref, own_ref, other_ref, weight_ref, query_ref, numer_ref, numer_grad_ref, local_grad_ref
):
    across, core = place_ref[0], place_ref[1]
    chips, _, width = own_ref.shape
    out_dir = jnp.zeros(numer_ref.shape, F32)
    for ahead in range(chips):
        chip = lax.rem(across + ahead, chips)
        for grad_ref, owner in ((own_ref, core), (other_ref, 1 - core)):
            start = pl.multiple_of((chip * 2 + owner) * width, width)
            out_dir = out_dir + dot(grad_ref[ahead], weight_ref[pl.ds(start, width), :], ((1,), (0,)))
    for head in range(width // HEAD_DIM):
        cols = head_cols(head)
        numer = numer_ref[:, cols]
        spread = jnp.sqrt(jnp.mean(numer * numer, axis=-1, keepdims=True) + 1e-06)
        normed = numer / spread
        here = out_dir[:, cols]
        along = jnp.mean(here * normed, axis=-1, keepdims=True)
        numer_grad = ((here - normed * along) / spread).astype(BF16)
        numer_grad_ref[:, cols] = numer_grad
        local_grad_ref[cols, :] = dot(query_ref[:, cols], numer_grad, ((0,), (0,))).astype(BF16)


def backward_kernel(
    query_ref, key_ref, value_ref, numer_grad_ref, prefix_ref, suffix_ref, query_out, key_out, value_out
):
    causal = causal_mask(query_ref.shape[0])
    for head in range(query_ref.shape[1] // HEAD_DIM):
        cols = head_cols(head)
        query, key, value = query_ref[:, cols], key_ref[:, cols], value_ref[:, cols]
        numer_grad, prefix, suffix = numer_grad_ref[:, cols], prefix_ref[cols, :], suffix_ref[cols, :]
        weights = jnp.where(causal, dot(query, key, ((1,), (1,))), 0.0).astype(BF16)
        pairs = jnp.where(causal, dot(numer_grad, value, ((1,), (1,))), 0.0).astype(BF16)
        query_out[:, cols] = (
            dot(pairs, key, ((1,), (0,))) + dot(numer_grad, prefix, ((1,), (1,)))
        ).astype(BF16)
        key_out[:, cols] = (
            dot(pairs, query, ((0,), (0,))) + dot(value, suffix, ((1,), (1,)))
        ).astype(BF16)
        value_out[:, cols] = (
            dot(weights, numer_grad, ((0,), (0,))) + dot(key, suffix, ((1,), (0,)))
        ).astype(BF16)


def permute(value, move):
    zh, zl, y, x, core = SIZES
    pairs = []
    for seq in range(zh * zl * y):
        for across in range(x):
            for half in range(core):
                to_across, to_half = move(across, half)
                pairs.append(
                    ((seq * x + across) * core + half, (seq * x + to_across % x) * core + to_half)
                )
    return lax.ppermute(value, AXES, pairs)


def per_device(queries, key_rows, values, out_weight, out_grad):
    rows, width = queries.shape
    group = lax.axis_index("zh").astype(jnp.int32).reshape(1)
    place = jnp.stack([lax.axis_index("x"), lax.axis_index("core")]).astype(jnp.int32)

    weight = out_weight.T
    copies = jnp.broadcast_to(weight[None], (SIZES[2],) + weight.shape)
    weight = lax.all_to_all(copies, "y", 0, 0, tiled=True).reshape(-1, width)
    weight = lax.all_gather(weight, ("zh", "zl"), axis=0, tiled=True)

    grads = [out_grad] + [
        permute(out_grad, lambda across, half, ahead=ahead: (across - ahead, half)) for ahead in (1, 2, 3)
    ]

    local_state = call(state_kernel, shape_of((width, HEAD_DIM), BF16), key_rows, values, name="state")
    prefix, own_grads, other_grads = outside_sum(local_state, group, False, grads)
    numer, attended = call(
        forward_kernel,
        (shape_of((rows, width), F32), shape_of((rows, width), BF16)),
        queries, key_rows, values, prefix,
        name="forward",
    )
    numer_grad, local_grad = call(
        middle_kernel,
        (shape_of((rows, width), BF16), shape_of((width, HEAD_DIM), BF16)),
        place, own_grads, other_grads, weight, queries, numer,
        smem=1,
        name="middle",
    )
    partial_out = dot(attended, weight, ((1,), (1,))).astype(BF16)
    mixed = lax.psum_scatter(partial_out, ("x", "core"), scatter_dimension=1, tiled=True)
    (suffix,) = outside_sum(local_grad, group, True)
    query_out, key_out, value_out = call(
        backward_kernel,
        (shape_of((rows, width), BF16),) * 3,
        queries, key_rows, values, numer_grad, prefix, suffix,
        name="backward",
    )
    return mixed, query_out, key_out, value_out


def solution(mesh):
    fine = Mesh(mesh.devices.reshape(SIZES), AXES)
    seq, head = ("zh", "zl", "y"), ("x", "core")
    rows = P(seq, head)
    return jax.shard_map(
        per_device,
        mesh=fine,
        in_specs=(rows, rows, rows, P(head, seq), rows),
        out_specs=(rows, rows, rows, rows),
        check_vma=False,
    )
```

time: 629 us -> 169 us (0.27)
  waiting for transfers between devices: 454 us -> 30.6 us
  other arithmetic: 133 us -> 0.08 us
  blocking collectives: 0 us -> 73.7 us
  starting transfers between devices: 0.2 us -> 30.8 us
  matrix products: 16.2 us -> 4.9 us
  Pallas kernels: 0 us -> 6.93 us
    all_gather x4 -> x1, waiting for transfers between devices: 453 us -> 10.9 us  [per_device(): weight = lax.all_gather(weight, ('zh', 'zl'), axis=0, tiled=True)]
    select_n x128 -> x0, other arithmetic: 133 us -> none  [hop(): return jnp.where(reached, new, before)]
    all_to_all x0 -> x5, blocking collectives: none -> 73.7 us  [the longest x2 29.3 us: outside_sum(): lax.all_to_all(sums, near, 0, 0, tiled=True).reshape(local.shape)]
    all_to_all x0 -> x2, starting transfers between devices: none -> 19 us  [the longest x1 12.4 us: outside_sum(): totals = lax.all_to_all(total, 'zh', 0, 0, tiled=True)]
    all_to_all x0 -> x2, waiting for transfers between devices: none -> 13.7 us  [the longest x1 13.7 us: outside_sum(): totals = lax.all_to_all(total, 'zh', 0, 0, tiled=True)]
    ppermute x0 -> x4, starting transfers between devices: none -> 11.8 us  [permute(): return lax.ppermute(value, AXES, pairs)]
    dot_general x14 -> x1, matrix products: 16.2 us -> 4.9 us  [dot(): lax.dot_general(left, right, (dims, ((), ())), preferred_element_type=F32)]
    pallas_call x0 -> x8, Pallas kernels: none -> 6.93 us  [call(): pl.pallas_call(body, out_shape=out_shape, in_specs=[pl.BlockSpec(memory_s...]
  transfers between devices with their start and end apart: 5 -> 8, of which waited for: 3 -> 5; matrix products, arithmetic and copies ran while one was open for 23% -> 0% of each run, Pallas kernels for 0% -> 4%
where the time goes in v1:
time: 169 us; the launch traced here: 168 us
  blocking collectives  73.7 us (44%)
  starting transfers between devices  30.8 us (18%)
  waiting for transfers between devices  30.6 us (18%)
  between operations  14.2 us (8%)
  Pallas kernels  6.93 us (4%)
  local copies, waits for them, and re-layouts  6.67 us (4%)
  matrix products  4.9 us (3%)
    all_to_all x2, blocking collectives, outside_sum(): lax.all_to_all(sums, near, 0, 0, tiled=True).reshape(local.shape)  29.3 us
    all_to_all x1, blocking collectives, outside_sum(): totals = lax.all_to_all(total, 'zh', 0, 0, tiled=True)  18.9 us
    all_to_all x1, blocking collectives, outside_sum(): pieces = lax.all_to_all(local.reshape(piece), near, 0, 0, tiled=True)  14.4 us
    all_to_all x1, waiting for transfers between devices, outside_sum(): totals = lax.all_to_all(total, 'zh', 0, 0, tiled=True)  13.7 us
    all_to_all x1, starting transfers between devices, outside_sum(): totals = lax.all_to_all(total, 'zh', 0, 0, tiled=True)  12.4 us
    ppermute x4, starting transfers between devices, permute(): return lax.ppermute(value, AXES, pairs)  11.8 us
    all_to_all x1, blocking collectives, per_device(): weight = lax.all_to_all(copies, 'y', 0, 0, tiled=True).reshape(-1, width)  11 us
    all_gather x1, waiting for transfers between devices, per_device(): weight = lax.all_gather(weight, ('zh', 'zl'), axis=0, tiled=True)  10.9 us
  transfers between devices with their start and end apart: 8, of which 5 were waited for; matrix products, arithmetic and copies ran while one was open for 0% of the time, Pallas kernels for 4%

profile of v1, /device:TPU:2, one launch (start us, length us, event | category | flops | bytes accessed | tf_op | source)
XLA Modules:
  0.0 167.9 jit_solution(12486277887015679426)
XLA Ops:
  7.2 0.0 copy-start.5
  7.2 0.0 copy-start.3
  7.2 0.0 copy-start.1
  7.2 0.0 all-gather.2.cloned.1.call-start
  7.2 0.9 broadcast_in_dim.2
  8.2 11.0 %all_to_all.35 = bf16[4,64,512]{2,1,0:T(8,128)(2,1)} all-to-all(bf16[4,64,512]{2,1,0:T(8,128)(2,1)S(1)} %broadcast_in_dim.2), channel_id=1, replica_groups=mesh['zh'=4,'zl'=4,'y'=4,'x'=4,'core'=2] {'y'}, dimensions={0} | all-to-all | bytes 524288 | tf_op jit(solution)/shard_map/all_to_all | solution.py:187
  19.2 0.0 all-gather.2.cloned.1.call-update
  19.2 0.0 copy-start.2
  19.3 0.9 copy-done.2
  20.2 0.0 copy-start.4
  20.2 0.9 copy-done.4
  21.1 0.9 state.1
  22.1 6.6 %all-to-all-start = ((bf16[16,32,128]{2,1,0:T(8,128)(2,1)}), bf16[16,32,128]{2,1,0:T(8,128)(2,1)S(1)}, u32[]{:S(2)}, u32[]{:S(2)}) async-start(bf16[16,32,128]{2,1,0:T(8,128)(2,1)} %bitcast.1), calls=%async_computation | async-start | bytes 262144 | tf_op jit(solution)/shard_map/all_to_all | solution.py:86
  28.7 4.0 %collective-permute-start.1 = (bf16[256,512]{1,0:T(8,128)(2,1)}, bf16[256,512]{1,0:T(8,128)(2,1)S(1)}, u32[]{:S(2)}, u32[]{:S(2)}) collective-permute-start(bf16[256,512]{1,0:T(8,128)(2,1)} %refs_1_.5), channel_id=1, source_target_pairs={{0,4},{1,5},{2,6},{3,7},{4,0},{5,1},{6,2},{7,3},{8,12},{9,13},{10,... | collective-permute-start | bytes 786440 | tf_op jit(solution)/shard_map/ppermute | solution.py:177
  32.7 3.3 %collective-permute-start = (bf16[256,512]{1,0:T(8,128)(2,1)}, bf16[256,512]{1,0:T(8,128)(2,1)S(1)}, u32[]{:S(2)}, u32[]{:S(2)}) collective-permute-start(bf16[256,512]{1,0:T(8,128)(2,1)} %refs_1_.5), channel_id=1, source_target_pairs={{0,6},{1,7},{2,0},{3,1},{4,2},{5,3},{6,4},{7,5},{8,14},{9,15},{10,... | collective-permute-start | bytes 786440 | tf_op jit(solution)/shard_map/ppermute | solution.py:177
  36.1 2.5 %collective-permute-start.2 = (bf16[256,512]{1,0:T(8,128)(2,1)}, bf16[256,512]{1,0:T(8,128)(2,1)S(1)}, u32[]{:S(2)}, u32[]{:S(2)}) collective-permute-start(bf16[256,512]{1,0:T(8,128)(2,1)} %refs_1_.5), channel_id=1, source_target_pairs={{0,2},{1,3},{2,4},{3,5},{4,6},{5,7},{6,0},{7,1},{8,10},{9,11},{10,... | collective-permute-start | bytes 786440 | tf_op jit(solution)/shard_map/ppermute | solution.py:177
  38.6 2.9 %collective-permute-done.1.refs_3_ = bf16[256,512]{1,0:T(8,128)(2,1)S(1)} collective-permute-done((bf16[256,512]{1,0:T(8,128)(2,1)}, bf16[256,512]{1,0:T(8,128)(2,1)S(1)}, u32[]{:S(2)}, u32[]{:S(2)}) %collective-permute-start.1) | collective-permute-done | bytes 262176 | tf_op jit(solution)/shard_map/ppermute | solution.py:177
  41.5 2.8 %collective-permute-done.refs_2_ = bf16[256,512]{1,0:T(8,128)(2,1)S(1)} collective-permute-done((bf16[256,512]{1,0:T(8,128)(2,1)}, bf16[256,512]{1,0:T(8,128)(2,1)S(1)}, u32[]{:S(2)}, u32[]{:S(2)}) %collective-permute-start) | collective-permute-done | bytes 262176 | tf_op jit(solution)/shard_map/ppermute | solution.py:177
  44.3 0.3 collective-permute-done.2.refs_4_
  44.6 0.0 all-to-all-done.refs_0_
  44.6 0.0 copy-start.7
  44.6 1.0 copy-done.7
  45.5 0.7 near_scan.2
  46.2 1.9 %collective-permute-start.3 = (bf16[4,256,512]{2,1,0:T(8,128)(2,1)S(1)}, bf16[4,256,512]{2,1,0:T(8,128)(2,1)S(1)}, u32[]{:S(2)}, u32[]{:S(2)}) collective-permute-start(bf16[4,256,512]{2,1,0:T(8,128)(2,1)S(1)} %get-tuple-element.18.refs_3_.refs_1_), channel_id=1, source_target_pairs={{0,1},{1,0},{2,3},{3,2},{4,5},{5,4},{6,7},{7,6},{8,9},{9,8},{10,11... | collective-permute-start | bytes 3145736 | tf_op jit(solution)/shard_map/ppermute | solution.py:177
  48.1 12.4 %all-to-all-start.1 = ((bf16[4,32,128]{2,1,0:T(8,128)(2,1)}), bf16[4,32,128]{2,1,0:T(8,128)(2,1)S(1)}, u32[]{:S(2)}, u32[]{:S(2)}) async-start(bf16[4,32,128]{2,1,0:T(8,128)(2,1)} %get-tuple-element.17), calls=%async_computation.1 | async-start | bytes 65536 | tf_op jit(solution)/shard_map/all_to_all | solution.py:95
  60.5 0.0 reduce-scatter.2.cloned.1.call-start
  60.5 13.7 %all-to-all-done.1.refs_2_ = bf16[4,32,128]{2,1,0:T(8,128)(2,1)S(1)} async-done(((bf16[4,32,128]{2,1,0:T(8,128)(2,1)}), bf16[4,32,128]{2,1,0:T(8,128)(2,1)S(1)}, u32[]{:S(2)}, u32[]{:S(2)}) %all-to-all-start.1) | async-done | bytes 32800 | tf_op jit(solution)/shard_map/all_to_all | solution.py:95
  74.2 0.0 collective-permute-done.3.refs_4_.refs_2_
  74.2 17.8 %all_to_all.36 = bf16[16,32,128]{2,1,0:T(8,128)(2,1)S(1)} all-to-all(bf16[16,32,128]{2,1,0:T(8,128)(2,1)S(1)} %far_scan.2), channel_id=1, replica_groups=mesh['zh'=4,'zl'=4,'y'=4,'x'=4,'core'=2] {'zl','y'}, dimensions={0} | all-to-all | bytes 262144 | tf_op jit(solution)/shard_map/all_to_all | solution.py:106
  92.0 0.0 copy-done.5
  92.0 0.0 copy-done.3
  92.0 0.0 copy-done.1
  92.0 0.8 forward.1
  92.8 0.0 copy-start.6
  92.8 0.7 copy-done.6
  93.5 10.9 %all-gather.2.cloned.1.call-done.refs_3_ = bf16[4096,512]{1,0:T(8,128)(2,1)} async-done(((bf16[256,512]{1,0:T(8,128)(2,1)}), bf16[4096,512]{1,0:T(8,128)(2,1)}) %all-gather.2.cloned.1.call-update) | async-done | bytes 4194320 | tf_op jit(solution)/shard_map/all_gather | solution.py:188
  104.4 4.9 %convolution_convert_fusion = bf16[256,4096]{1,0:T(8,128)(2,1)} fusion(bf16[256,512]{1,0:T(8,128)(2,1)} %copy-done.6, bf16[4096,512]{1,0:T(8,128)(2,1)} %all-gather.2.cloned.1.call-done.refs_3_), kind=kOutput, calls=%fused_computation | convolution fusion | flops 1074790400 | bytes 6553600 | tf_op jit(solution)/shard_map/dot_general | solution.py:18
  109.3 0.0 reduce-scatter.2.cloned.1.call-update
  109.4 0.1 pad_add_fusion.refs_0_
  109.4 0.0 copy-start
  109.4 2.2 %copy-done = bf16[4096,512]{1,0:T(8,128)(2,1)S(1)} copy-done((bf16[4096,512]{1,0:T(8,128)(2,1)S(1)}, bf16[4096,512]{1,0:T(8,128)(2,1)}, u32[]{:S(2)}) %copy-start) | copy-done | bytes 4194328
  111.6 2.3 %middle.1 = (bf16[256,512]{1,0:T(8,128)(2,1)S(1)}, bf16[512,128]{1,0:T(8,128)(2,1)S(1)}) custom-call(s32[2]{0:T(128)S(1)} %pad_add_fusion.refs_0_, bf16[4,256,512]{2,1,0:T(8,128)(2,1)S(1)} %get-tuple-element.18.refs_3_.refs_1_, bf16[4,256,512]{2,1,0:T(8,128)(2,1)S(1)} %collective-permute-done.3.refs_4_.refs_2_, bf16[4096,512]{1,0:T(8,128)(2,1)S(1)} %copy-done, ...), custom_call_target="tpu_custom_call" | custom-call | tf_op jit(solution)/shard_map/middle/pallas_call | solution.py:33
  113.9 14.4 %all_to_all.37.refs_0_ = bf16[16,32,128]{2,1,0:T(8,128)(2,1)S(1)} all-to-all(bf16[16,32,128]{2,1,0:T(8,128)(2,1)S(1)} %bitcast.14), channel_id=1, replica_groups=mesh['zh'=4,'zl'=4,'y'=4,'x'=4,'core'=2] {'zl','y'}, dimensions={0} | all-to-all | bytes 262144 | tf_op jit(solution)/shard_map/all_to_all | solution.py:86
  128.3 18.9 %all_to_all.38.refs_2_ = bf16[4,32,128]{2,1,0:T(8,128)(2,1)S(1)} all-to-all(bf16[4,32,128]{2,1,0:T(8,128)(2,1)S(1)} %get-tuple-element.24), channel_id=1, replica_groups=mesh['zh'=4,'zl'=4,'y'=4,'x'=4,'core'=2] {'zh'}, dimensions={0} | all-to-all | bytes 65536 | tf_op jit(solution)/shard_map/all_to_all | solution.py:95
  147.3 11.5 %all_to_all.39 = bf16[16,32,128]{2,1,0:T(8,128)(2,1)S(1)} all-to-all(bf16[16,32,128]{2,1,0:T(8,128)(2,1)S(1)} %far_scan.3), channel_id=1, replica_groups=mesh['zh'=4,'zl'=4,'y'=4,'x'=4,'core'=2] {'zl','y'}, dimensions={0} | all-to-all | bytes 262144 | tf_op jit(solution)/shard_map/all_to_all | solution.py:106
  158.8 2.2 %backward.1 = (bf16[256,512]{1,0:T(8,128)(2,1)}, bf16[256,512]{1,0:T(8,128)(2,1)}, bf16[256,512]{1,0:T(8,128)(2,1)}) custom-call(bf16[256,512]{1,0:T(8,128)(2,1)S(1)} %copy-done.1, bf16[256,512]{1,0:T(8,128)(2,1)S(1)} %copy-done.3, bf16[256,512]{1,0:T(8,128)(2,1)S(1)} %copy-done.5, bf16[256,512]{1,0:T(8,128)(2,1)S(1)} %get-tuple-element.21.refs_3_, ...), custom_call_target="tpu_custom_call" | custom-call | tf_op jit(solution)/shard_map/backward/pallas_call | solution.py:33
  161.0 0.0 reduce-scatter.2.cloned.1.call-done
  (3 shorter events, 0.1 us)
Async XLA Ops:
  7.2 84.9 %copy-start.5 = (bf16[256,512]{1,0:T(8,128)(2,1)S(1)}, bf16[256,512]{1,0:T(8,128)(2,1)}, u32[]{:S(2)}) copy-start(bf16[256,512]{1,0:T(8,128)(2,1)} %refs_2_.3) | copy-start | bytes 786436
  7.2 84.9 %copy-start.3 = (bf16[256,512]{1,0:T(8,128)(2,1)S(1)}, bf16[256,512]{1,0:T(8,128)(2,1)}, u32[]{:S(2)}) copy-start(bf16[256,512]{1,0:T(8,128)(2,1)} %refs_1_.7) | copy-start | bytes 786436
  7.2 84.8 %copy-start.1 = (bf16[256,512]{1,0:T(8,128)(2,1)S(1)}, bf16[256,512]{1,0:T(8,128)(2,1)}, u32[]{:S(2)}) copy-start(bf16[256,512]{1,0:T(8,128)(2,1)} %refs_0_.5) | copy-start | bytes 786436
  7.2 97.2 %all-gather.2.cloned.1.call-start = ((), (), s32[]{:S(2)}) async-start(), calls=%async_computation.8 | async-start | bytes 4456448 | tf_op jit(solution)/shard_map/all_gather | solution.py:188
  19.2 1.0 copy-start.2
  20.2 0.9 copy-start.4
  22.1 22.5 %all-to-all-start = ((bf16[16,32,128]{2,1,0:T(8,128)(2,1)}), bf16[16,32,128]{2,1,0:T(8,128)(2,1)S(1)}, u32[]{:S(2)}, u32[]{:S(2)}) async-start(bf16[16,32,128]{2,1,0:T(8,128)(2,1)} %bitcast.1), calls=%async_computation | async-start | bytes 262144 | tf_op jit(solution)/shard_map/all_to_all | solution.py:86
  28.7 12.8 %collective-permute-start.1 = (bf16[256,512]{1,0:T(8,128)(2,1)}, bf16[256,512]{1,0:T(8,128)(2,1)S(1)}, u32[]{:S(2)}, u32[]{:S(2)}) collective-permute-start(bf16[256,512]{1,0:T(8,128)(2,1)} %refs_1_.5), channel_id=1, source_target_pairs={{0,4},{1,5},{2,6},{3,7},{4,0},{5,1},{6,2},{7,3},{8,12},{9,13},{10,... | collective-permute-start | bytes 786440 | tf_op jit(solution)/shard_map/ppermute | solution.py:177
  32.7 11.5 %collective-permute-start = (bf16[256,512]{1,0:T(8,128)(2,1)}, bf16[256,512]{1,0:T(8,128)(2,1)S(1)}, u32[]{:S(2)}, u32[]{:S(2)}) collective-permute-start(bf16[256,512]{1,0:T(8,128)(2,1)} %refs_1_.5), channel_id=1, source_target_pairs={{0,6},{1,7},{2,0},{3,1},{4,2},{5,3},{6,4},{7,5},{8,14},{9,15},{10,... | collective-permute-start | bytes 786440 | tf_op jit(solution)/shard_map/ppermute | solution.py:177
  36.1 8.5 %collective-permute-start.2 = (bf16[256,512]{1,0:T(8,128)(2,1)}, bf16[256,512]{1,0:T(8,128)(2,1)S(1)}, u32[]{:S(2)}, u32[]{:S(2)}) collective-permute-start(bf16[256,512]{1,0:T(8,128)(2,1)} %refs_1_.5), channel_id=1, source_target_pairs={{0,2},{1,3},{2,4},{3,5},{4,6},{5,7},{6,0},{7,1},{8,10},{9,11},{10,... | collective-permute-start | bytes 786440 | tf_op jit(solution)/shard_map/ppermute | solution.py:177
  44.6 1.0 copy-start.7
  46.2 28.0 %collective-permute-start.3 = (bf16[4,256,512]{2,1,0:T(8,128)(2,1)S(1)}, bf16[4,256,512]{2,1,0:T(8,128)(2,1)S(1)}, u32[]{:S(2)}, u32[]{:S(2)}) collective-permute-start(bf16[4,256,512]{2,1,0:T(8,128)(2,1)S(1)} %get-tuple-element.18.refs_3_.refs_1_), channel_id=1, source_target_pairs={{0,1},{1,0},{2,3},{3,2},{4,5},{5,4},{6,7},{7,6},{8,9},{9,8},{10,11... | collective-permute-start | bytes 3145736 | tf_op jit(solution)/shard_map/ppermute | solution.py:177
  48.1 26.1 %all-to-all-start.1 = ((bf16[4,32,128]{2,1,0:T(8,128)(2,1)}), bf16[4,32,128]{2,1,0:T(8,128)(2,1)S(1)}, u32[]{:S(2)}, u32[]{:S(2)}) async-start(bf16[4,32,128]{2,1,0:T(8,128)(2,1)} %get-tuple-element.17), calls=%async_computation.1 | async-start | bytes 65536 | tf_op jit(solution)/shard_map/all_to_all | solution.py:95
  60.5 100.5 %reduce-scatter.2.cloned.1.call-start = ((), (), s32[]{:S(2)}) async-start(), calls=%async_computation.9 | async-start | bytes 2359296 | tf_op jit(solution)/shard_map/reduce_scatter | solution.py:210
  92.8 0.7 copy-start.6
  109.4 2.2 %copy-start = (bf16[4096,512]{1,0:T(8,128)(2,1)S(1)}, bf16[4096,512]{1,0:T(8,128)(2,1)}, u32[]{:S(2)}) copy-start(bf16[4096,512]{1,0:T(8,128)(2,1)} %all-gather.2.cloned.1.call-done.refs_3_) | copy-start | bytes 12582916
Sparse Core Ops, SparseCore 0:
  19.4 85.0 all-gather.1
  109.5 32.7 reduce-scatter.1

commit v2 on v1

--- a/solution.py
+++ b/solution.py
@@ -11,7 +11,7 @@
 BF16 = jnp.bfloat16
 AXES = ("zh", "zl", "y", "x", "core")
 SIZES = (4, 4, 4, 4, 2)
-PARAMS = pltpu.CompilerParams(vmem_limit_bytes=40 * 1024 * 1024)
+PARAMS = pltpu.CompilerParams(vmem_limit_bytes=24 * 1024 * 1024)
 
 
 def dot(left, right, dims):
@@ -106,7 +106,7 @@
     return lax.all_to_all(sums, near, 0, 0, tiled=True).reshape(local.shape), *stack
 
 
-def forward_kernel(query_ref, key_ref, value_ref, prefix_ref, numer_ref, attended_ref):
+def forward_kernel(query_ref, key_ref, value_ref, prefix_ref, numer_ref):
     causal = causal_mask(query_ref.shape[0])
     for head in range(query_ref.shape[1] // HEAD_DIM):
         cols = head_cols(head)
@@ -115,53 +115,120 @@
         weights = jnp.where(causal, scores, 0.0).astype(BF16)
         numer = dot(weights, value_ref[:, cols], ((1,), (0,)))
         numer = numer + dot(query, prefix_ref[cols, :], ((1,), (0,)))
+        numer_ref[:, cols] = numer
+
+
+def middle_kernel(
+    place_ref, own_hbm, other_hbm, weight_hbm, query_ref, numer_ref,
+    numer_grad_ref, local_grad_ref, partial_hbm,
+    weight_ref, grad_ref, attended_ref, out_dir_ref, partial_ref, in_sems, grad_sems, out_sems,
+):
+    chips, rows, width = own_hbm.shape
+    across, core = place_ref[0], place_ref[1]
+
+    def share(step):
+        owner = core if step % 2 == 0 else 1 - core
+        start = (lax.rem(across + step // 2, chips) * 2 + owner) * width
+        return pl.ds(pl.multiple_of(start, width), width)
+
+    fetches = [
+        pltpu.make_async_copy(weight_hbm.at[share(step), :], weight_ref.at[step], in_sems.at[step])
+        for step in range(2 * chips)
+    ]
+    grads = [
+        pltpu.make_async_copy(
+            (own_hbm if step % 2 == 0 else other_hbm).at[step // 2], grad_ref.at[step], grad_sems.at[step]
+        )
+        for step in range(2 * chips)
+    ]
+    for fetch, grad in zip(fetches, grads):
+        fetch.start()
+        grad.start()
+    for head in range(width // HEAD_DIM):
+        cols = head_cols(head)
+        numer = numer_ref[:, cols]
         spread = jnp.sqrt(jnp.mean(numer * numer, axis=-1, keepdims=True) + 1e-06)
-        numer_ref[:, cols] = numer
         attended_ref[:, cols] = (numer / spread).astype(BF16)
-
-
-def middle_kernel(
-    place_ref, own_ref, other_ref, weight_ref, query_ref, numer_ref, numer_grad_ref, local_grad_ref
-):
-    across, core = place_ref[0], place_ref[1]
-    chips, _, width = own_ref.shape
-    out_dir = jnp.zeros(numer_ref.shape, F32)
-    for ahead in range(chips):
-        chip = lax.rem(across + ahead, chips)
-        for grad_ref, owner in ((own_ref, core), (other_ref, 1 - core)):
-            start = pl.multiple_of((chip * 2 + owner) * width, width)
-            out_dir = out_dir + dot(grad_ref[ahead], weight_ref[pl.ds(start, width), :], ((1,), (0,)))
+    sends = []
+    for step in range(2 * chips):
+        fetches[step].wait()
+        grads[step].wait()
+        term = dot(grad_ref[step], weight_ref[step], ((1,), (0,)))
+        if step == 0:
+            out_dir_ref[...] = term
+        else:
+            out_dir_ref[...] += term
+        partial_ref[step] = dot(attended_ref[...], weight_ref[step], ((1,), (1,))).astype(BF16)
+        sends.append(
+            pltpu.make_async_copy(partial_ref.at[step], partial_hbm.at[:, share(step)], out_sems.at[step])
+        )
+        sends[step].start()
     for head in range(width // HEAD_DIM):
         cols = head_cols(head)
         numer = numer_ref[:, cols]
         spread = jnp.sqrt(jnp.mean(numer * numer, axis=-1, keepdims=True) + 1e-06)
         normed = numer / spread
-        here = out_dir[:, cols]
-        along = jnp.mean(here * normed, axis=-1, keepdims=True)
-        numer_grad = ((here - normed * along) / spread).astype(BF16)
+        direction = out_dir_ref[:, cols]
+        along = jnp.mean(direction * normed, axis=-1, keepdims=True)
+        numer_grad = ((direction - normed * along) / spread).astype(BF16)
         numer_grad_ref[:, cols] = numer_grad
         local_grad_ref[cols, :] = dot(query_ref[:, cols], numer_grad, ((0,), (0,))).astype(BF16)
+    for send in sends:
+        send.wait()
+
+
+def middle(place, own, other, weight, queries, numer):
+    chips, rows, width = own.shape
+    shares = 2 * chips
+    vmem = pl.BlockSpec(memory_space=pltpu.VMEM)
+    hbm = pl.BlockSpec(memory_space=pltpu.HBM)
+    return pl.pallas_call(
+        middle_kernel,
+        out_shape=(
+            shape_of((rows, width), BF16),
+            shape_of((width, HEAD_DIM), BF16),
+            shape_of((rows, shares * width), BF16),
+        ),
+        in_specs=[pl.BlockSpec(memory_space=pltpu.SMEM), hbm, hbm, hbm, vmem, vmem],
+        out_specs=[vmem, vmem, hbm],
+        scratch_shapes=[
+            pltpu.VMEM((shares, width, width), BF16),
+            pltpu.VMEM((shares, rows, width), BF16),
+            pltpu.VMEM((rows, width), BF16),
+            pltpu.VMEM((rows, width), F32),
+            pltpu.VMEM((shares, rows, width), BF16),
+            pltpu.SemaphoreType.DMA((shares,)),
+            pltpu.SemaphoreType.DMA((shares,)),
+            pltpu.SemaphoreType.DMA((shares,)),
+        ],
+        compiler_params=pltpu.CompilerParams(vmem_limit_bytes=60 * 1024 * 1024),
+        name="middle",
+    )(place, own, other, weight, queries, numer)
 
 
 def backward_kernel(
-    query_ref, key_ref, value_ref, numer_grad_ref, prefix_ref, suffix_ref, query_out, key_out, value_out
+    query_ref, key_ref, value_ref, numer_grad_ref, prefix_ref, query_out, key_part, value_part
 ):
     causal = causal_mask(query_ref.shape[0])
     for head in range(query_ref.shape[1] // HEAD_DIM):
         cols = head_cols(head)
         query, key, value = query_ref[:, cols], key_ref[:, cols], value_ref[:, cols]
-        numer_grad, prefix, suffix = numer_grad_ref[:, cols], prefix_ref[cols, :], suffix_ref[cols, :]
+        numer_grad = numer_grad_ref[:, cols]
         weights = jnp.where(causal, dot(query, key, ((1,), (1,))), 0.0).astype(BF16)
         pairs = jnp.where(causal, dot(numer_grad, value, ((1,), (1,))), 0.0).astype(BF16)
         query_out[:, cols] = (
-            dot(pairs, key, ((1,), (0,))) + dot(numer_grad, prefix, ((1,), (1,)))
+            dot(pairs, key, ((1,), (0,))) + dot(numer_grad, prefix_ref[cols, :], ((1,), (1,)))
         ).astype(BF16)
-        key_out[:, cols] = (
-            dot(pairs, query, ((0,), (0,))) + dot(value, suffix, ((1,), (1,)))
-        ).astype(BF16)
-        value_out[:, cols] = (
-            dot(weights, numer_grad, ((0,), (0,))) + dot(key, suffix, ((1,), (0,)))
-        ).astype(BF16)
+        key_part[:, cols] = dot(pairs, query, ((0,), (0,)))
+        value_part[:, cols] = dot(weights, numer_grad, ((0,), (0,)))
+
+
+def suffix_kernel(key_ref, value_ref, suffix_ref, key_part, value_part, key_out, value_out):
+    for head in range(key_ref.shape[1] // HEAD_DIM):
+        cols = head_cols(head)
+        suffix = suffix_ref[cols, :]
+        key_out[:, cols] = (key_part[:, cols] + dot(value_ref[:, cols], suffix, ((1,), (1,)))).astype(BF16)
+        value_out[:, cols] = (value_part[:, cols] + dot(key_ref[:, cols], suffix, ((1,), (0,)))).astype(BF16)
 
 
 def permute(value, move):
@@ -193,27 +260,23 @@
 
     local_state = call(state_kernel, shape_of((width, HEAD_DIM), BF16), key_rows, values, name="state")
     prefix, own_grads, other_grads = outside_sum(local_state, group, False, grads)
-    numer, attended = call(
-        forward_kernel,
-        (shape_of((rows, width), F32), shape_of((rows, width), BF16)),
-        queries, key_rows, values, prefix,
-        name="forward",
-    )
-    numer_grad, local_grad = call(
-        middle_kernel,
-        (shape_of((rows, width), BF16), shape_of((width, HEAD_DIM), BF16)),
-        place, own_grads, other_grads, weight, queries, numer,
-        smem=1,
-        name="middle",
-    )
-    partial_out = dot(attended, weight, ((1,), (1,))).astype(BF16)
+    numer = call(
+        forward_kernel, shape_of((rows, width), F32), queries, key_rows, values, prefix, name="forward"
+    )
+    numer_grad, local_grad, partial_out = middle(place, own_grads, other_grads, weight, queries, numer)
     mixed = lax.psum_scatter(partial_out, ("x", "core"), scatter_dimension=1, tiled=True)
     (suffix,) = outside_sum(local_grad, group, True)
-    query_out, key_out, value_out = call(
+    query_out, key_part, value_part = call(
         backward_kernel,
-        (shape_of((rows, width), BF16),) * 3,
-        queries, key_rows, values, numer_grad, prefix, suffix,
+        (shape_of((rows, width), BF16),) + (shape_of((rows, width), F32),) * 2,
+        queries, key_rows, values, numer_grad, prefix,
         name="backward",
+    )
+    key_out, value_out = call(
+        suffix_kernel,
+        (shape_of((rows, width), BF16),) * 2,
+        key_rows, values, suffix, key_part, value_part,
+        name="suffix",
     )
     return mixed, query_out, key_out, value_out
 

time: 169 us -> 167 us (0.988)
  blocking collectives: 73.7 us -> 45.4 us
  waiting for transfers between devices: 30.6 us -> 45.5 us
  starting transfers between devices: 30.8 us -> 41 us
  Pallas kernels: 6.93 us -> 14.4 us
  matrix products: 4.9 us -> 0 us
    all_to_all x2 -> x0, blocking collectives: 29.3 us -> none  [outside_sum(): lax.all_to_all(sums, near, 0, 0, tiled=True).reshape(local.shape)]
    all_to_all x0 -> x2, waiting for transfers between devices: none -> 16.7 us  [outside_sum(): lax.all_to_all(sums, near, 0, 0, tiled=True).reshape(local.shape)]
    all_to_all x0 -> x2, starting transfers between devices: none -> 10.1 us  [outside_sum(): lax.all_to_all(sums, near, 0, 0, tiled=True).reshape(local.shape)]
    pallas_call x0 -> x1, Pallas kernels: none -> 7.55 us  [middle(): pl.pallas_call(middle_kernel, out_shape=(shape_of((rows, width), BF16), s...]
    dot_general x1 -> x0, matrix products: 4.9 us -> none  [dot(): lax.dot_general(left, right, (dims, ((), ())), preferred_element_type=F32)]
    all_gather x1, waiting for transfers between devices: 10.9 us -> 9.16 us  [per_device(): weight = lax.all_gather(weight, ('zh', 'zl'), axis=0, tiled=True)]
    unnamed x16 -> x22, local copies, waits for them, and re-layouts: 5.75 us -> 4.69 us
  transfers between devices with their start and end apart: 8 -> 10, of which waited for: 5 -> 7; matrix products, arithmetic and copies ran while one was open for 0% -> 0% of each run, Pallas kernels for 4% -> 4%
where the time goes in v2:
time: 167 us
  waiting for transfers between devices  45.5 us (27%)
  blocking collectives  45.4 us (27%)
  starting transfers between devices  41 us (25%)
  Pallas kernels  14.4 us (9%)
  between operations  14.2 us (9%)
  local copies, waits for them, and re-layouts  5.6 us (3%)
    all_to_all x1, blocking collectives, outside_sum(): totals = lax.all_to_all(total, 'zh', 0, 0, tiled=True)  19.1 us
    all_to_all x2, waiting for transfers between devices, outside_sum(): lax.all_to_all(sums, near, 0, 0, tiled=True).reshape(local.shape)  16.7 us
    all_to_all x1, blocking collectives, outside_sum(): pieces = lax.all_to_all(local.reshape(piece), near, 0, 0, tiled=True)  15.2 us
    all_to_all x1, waiting for transfers between devices, outside_sum(): totals = lax.all_to_all(total, 'zh', 0, 0, tiled=True)  13.7 us
    all_to_all x1, starting transfers between devices, outside_sum(): totals = lax.all_to_all(total, 'zh', 0, 0, tiled=True)  12.4 us
    ppermute x4, starting transfers between devices, permute(): return lax.ppermute(value, AXES, pairs)  11.8 us
    all_to_all x1, blocking collectives, per_device(): weight = lax.all_to_all(copies, 'y', 0, 0, tiled=True).reshape(-1, width)  11 us
    all_to_all x2, starting transfers between devices, outside_sum(): lax.all_to_all(sums, near, 0, 0, tiled=True).reshape(local.shape)  10.1 us
  transfers between devices with their start and end apart: 10, of which 7 were waited for; matrix products, arithmetic and copies ran while one was open for 0% of the time, Pallas kernels for 4%

profile of v2, /device:TPU:2, one launch (start us, length us, event | category | flops | bytes accessed | tf_op | source)
XLA Modules:
  0.0 166.6 jit_solution(3158543136556645310)
XLA Ops:
  7.2 0.0 copy-start.5
  7.2 0.0 copy-start.3
  7.2 0.0 copy-start.6
  7.2 0.0 all-gather.2.cloned.1.call-start
  7.2 0.9 broadcast_in_dim.2
  8.2 11.0 %all_to_all.35 = bf16[4,64,512]{2,1,0:T(8,128)(2,1)} all-to-all(bf16[4,64,512]{2,1,0:T(8,128)(2,1)S(1)} %broadcast_in_dim.2), channel_id=1, replica_groups=mesh['zh'=4,'zl'=4,'y'=4,'x'=4,'core'=2] {'y'}, dimensions={0} | all-to-all | bytes 524288 | tf_op jit(solution)/shard_map/all_to_all | solution.py:254
  19.2 0.0 all-gather.2.cloned.1.call-update
  19.2 0.0 copy-start.2
  19.3 0.9 copy-done.2
  20.2 0.9 copy-done.4
  21.1 0.9 state.1
  22.1 6.6 %all-to-all-start = ((bf16[16,32,128]{2,1,0:T(8,128)(2,1)}), bf16[16,32,128]{2,1,0:T(8,128)(2,1)S(1)}, u32[]{:S(2)}, u32[]{:S(2)}) async-start(bf16[16,32,128]{2,1,0:T(8,128)(2,1)} %bitcast.2), calls=%async_computation | async-start | bytes 262144 | tf_op jit(solution)/shard_map/all_to_all | solution.py:86
  28.7 4.0 %collective-permute-start.1 = (bf16[256,512]{1,0:T(8,128)(2,1)}, bf16[256,512]{1,0:T(8,128)(2,1)S(1)}, u32[]{:S(2)}, u32[]{:S(2)}) collective-permute-start(bf16[256,512]{1,0:T(8,128)(2,1)} %refs_1_.6), channel_id=1, source_target_pairs={{0,4},{1,5},{2,6},{3,7},{4,0},{5,1},{6,2},{7,3},{8,12},{9,13},{10,... | collective-permute-start | bytes 786440 | tf_op jit(solution)/shard_map/ppermute | solution.py:244
  32.7 3.3 %collective-permute-start = (bf16[256,512]{1,0:T(8,128)(2,1)}, bf16[256,512]{1,0:T(8,128)(2,1)S(1)}, u32[]{:S(2)}, u32[]{:S(2)}) collective-permute-start(bf16[256,512]{1,0:T(8,128)(2,1)} %refs_1_.6), channel_id=1, source_target_pairs={{0,6},{1,7},{2,0},{3,1},{4,2},{5,3},{6,4},{7,5},{8,14},{9,15},{10,... | collective-permute-start | bytes 786440 | tf_op jit(solution)/shard_map/ppermute | solution.py:244
  36.1 2.5 %collective-permute-start.2 = (bf16[256,512]{1,0:T(8,128)(2,1)}, bf16[256,512]{1,0:T(8,128)(2,1)S(1)}, u32[]{:S(2)}, u32[]{:S(2)}) collective-permute-start(bf16[256,512]{1,0:T(8,128)(2,1)} %refs_1_.6), channel_id=1, source_target_pairs={{0,2},{1,3},{2,4},{3,5},{4,6},{5,7},{6,0},{7,1},{8,10},{9,11},{10,... | collective-permute-start | bytes 786440 | tf_op jit(solution)/shard_map/ppermute | solution.py:244
  38.6 2.9 %collective-permute-done.1.refs_3_ = bf16[256,512]{1,0:T(8,128)(2,1)S(1)} collective-permute-done((bf16[256,512]{1,0:T(8,128)(2,1)}, bf16[256,512]{1,0:T(8,128)(2,1)S(1)}, u32[]{:S(2)}, u32[]{:S(2)}) %collective-permute-start.1) | collective-permute-done | bytes 262176 | tf_op jit(solution)/shard_map/ppermute | solution.py:244
  41.5 2.8 %collective-permute-done.refs_2_ = bf16[256,512]{1,0:T(8,128)(2,1)S(1)} collective-permute-done((bf16[256,512]{1,0:T(8,128)(2,1)}, bf16[256,512]{1,0:T(8,128)(2,1)S(1)}, u32[]{:S(2)}, u32[]{:S(2)}) %collective-permute-start) | collective-permute-done | bytes 262176 | tf_op jit(solution)/shard_map/ppermute | solution.py:244
  44.3 0.3 collective-permute-done.2.refs_4_
  44.6 0.0 all-to-all-done.refs_0_
  44.6 1.0 copy-done.9
  45.5 0.7 near_scan.2
  46.2 1.9 %collective-permute-start.3 = (bf16[4,256,512]{2,1,0:T(8,128)(2,1)S(1)}, bf16[4,256,512]{2,1,0:T(8,128)(2,1)S(1)}, u32[]{:S(2)}, u32[]{:S(2)}) collective-permute-start(bf16[4,256,512]{2,1,0:T(8,128)(2,1)S(1)} %get-tuple-element.17.refs_3_.own_hbm), channel_id=1, source_target_pairs={{0,1},{1,0},{2,3},{3,2},{4,5},{5,4},{6,7},{7,6},{8,9},{9,8},{10,11... | collective-permute-start | bytes 3145736 | tf_op jit(solution)/shard_map/ppermute | solution.py:244
  48.1 12.4 %all-to-all-start.2 = ((bf16[4,32,128]{2,1,0:T(8,128)(2,1)}), bf16[4,32,128]{2,1,0:T(8,128)(2,1)S(1)}, u32[]{:S(2)}, u32[]{:S(2)}) async-start(bf16[4,32,128]{2,1,0:T(8,128)(2,1)} %get-tuple-element.19), calls=%async_computation.2 | async-start | bytes 65536 | tf_op jit(solution)/shard_map/all_to_all | solution.py:95
  60.5 13.7 %all-to-all-done.2.refs_2_ = bf16[4,32,128]{2,1,0:T(8,128)(2,1)S(1)} async-done(((bf16[4,32,128]{2,1,0:T(8,128)(2,1)}), bf16[4,32,128]{2,1,0:T(8,128)(2,1)S(1)}, u32[]{:S(2)}, u32[]{:S(2)}) %all-to-all-start.2) | async-done | bytes 32800 | tf_op jit(solution)/shard_map/all_to_all | solution.py:95
  74.2 0.0 collective-permute-done.3.refs_4_.other_hbm
  74.2 0.7 far_scan.2
  74.9 6.6 %all-to-all-start.3 = ((bf16[16,32,128]{2,1,0:T(8,128)(2,1)}), bf16[16,32,128]{2,1,0:T(8,128)(2,1)S(1)}, u32[]{:S(2)}, u32[]{:S(2)}) async-start(bf16[16,32,128]{2,1,0:T(8,128)(2,1)} %far_scan.2), calls=%async_computation.3 | async-start | bytes 262144 | tf_op jit(solution)/shard_map/all_to_all | solution.py:106
  81.6 0.0 reduce-scatter.2.cloned.1.call-start
  81.6 0.6 pad_add_fusion.place_ref
  82.2 10.8 %all-to-all-done.3 = bf16[16,32,128]{2,1,0:T(8,128)(2,1)S(1)} async-done(((bf16[16,32,128]{2,1,0:T(8,128)(2,1)}), bf16[16,32,128]{2,1,0:T(8,128)(2,1)S(1)}, u32[]{:S(2)}, u32[]{:S(2)}) %all-to-all-start.3) | async-done | bytes 131104 | tf_op jit(solution)/shard_map/all_to_all | solution.py:106
  93.0 0.0 copy-done.5
  93.0 0.0 copy-done.3
  93.0 0.0 copy-done.6
  93.0 0.7 forward.1.numer_ref
  93.7 0.9 copy-done.8
  94.5 9.2 %all-gather.2.cloned.1.call-done.weight_hbm = bf16[4096,512]{1,0:T(8,128)(2,1)} async-done(((bf16[256,512]{1,0:T(8,128)(2,1)}), bf16[4096,512]{1,0:T(8,128)(2,1)}) %all-gather.2.cloned.1.call-update) | async-done | bytes 4194320 | tf_op jit(solution)/shard_map/all_gather | solution.py:255
  103.7 0.0 copy-done.1
  103.7 7.6 %middle.1 = (bf16[256,512]{1,0:T(8,128)(2,1)}, bf16[512,128]{1,0:T(8,128)(2,1)}, bf16[256,4096]{1,0:T(8,128)(2,1)}) custom-call(s32[2]{0:T(128)} %pad_add_fusion.place_ref, bf16[4,256,512]{2,1,0:T(8,128)(2,1)} %copy-done, bf16[4,256,512]{2,1,0:T(8,128)(2,1)} %copy-done.1, bf16[4096,512]{1,0:T(8,128)(2,1)} %all-gather.2.cloned.1.call-done.weight_hbm, ...), custom_call_target="tpu_custom_call" | custom-call | tf_op jit(solution)/shard_map/middle/pallas_call | solution.py:185
  111.3 0.0 reduce-scatter.2.cloned.1.call-update
  111.3 15.2 %all_to_all.36.refs_0_ = bf16[16,32,128]{2,1,0:T(8,128)(2,1)S(1)} all-to-all(bf16[16,32,128]{2,1,0:T(8,128)(2,1)} %bitcast.13), channel_id=1, replica_groups=mesh['zh'=4,'zl'=4,'y'=4,'x'=4,'core'=2] {'zl','y'}, dimensions={0} | all-to-all | bytes 262144 | tf_op jit(solution)/shard_map/all_to_all | solution.py:86
  126.5 19.1 %all_to_all.37.refs_2_ = bf16[4,32,128]{2,1,0:T(8,128)(2,1)S(1)} all-to-all(bf16[4,32,128]{2,1,0:T(8,128)(2,1)S(1)} %get-tuple-element.25), channel_id=1, replica_groups=mesh['zh'=4,'zl'=4,'y'=4,'x'=4,'core'=2] {'zh'}, dimensions={0} | all-to-all | bytes 65536 | tf_op jit(solution)/shard_map/all_to_all | solution.py:95
  145.6 0.7 far_scan.3
  146.3 3.5 %all-to-all-start.6 = ((bf16[16,32,128]{2,1,0:T(8,128)(2,1)}), bf16[16,32,128]{2,1,0:T(8,128)(2,1)S(1)}, u32[]{:S(2)}, u32[]{:S(2)}) async-start(bf16[16,32,128]{2,1,0:T(8,128)(2,1)} %far_scan.3), calls=%async_computation.7 | async-start | bytes 262144 | tf_op jit(solution)/shard_map/all_to_all | solution.py:106
  149.8 0.0 copy-start.10
  149.8 0.9 copy-done.10
  150.8 2.0 %backward.1 = (bf16[256,512]{1,0:T(8,128)(2,1)}, f32[256,512]{1,0:T(8,128)S(1)}, f32[256,512]{1,0:T(8,128)S(1)}) custom-call(bf16[256,512]{1,0:T(8,128)(2,1)S(1)} %copy-done.7, bf16[256,512]{1,0:T(8,128)(2,1)S(1)} %copy-done.3, bf16[256,512]{1,0:T(8,128)(2,1)S(1)} %copy-done.5, bf16[256,512]{1,0:T(8,128)(2,1)S(1)} %copy-done.10, bf16[512,128]{1,0:T(8,128)(2,1)S(1)} %bitcast.10), custom_call_target="tpu_custom_call" | custom-call | tf_op jit(solution)/shard_map/backward/pallas_call | solution.py:33
  152.8 5.9 %all-to-all-done.6 = bf16[16,32,128]{2,1,0:T(8,128)(2,1)S(1)} async-done(((bf16[16,32,128]{2,1,0:T(8,128)(2,1)}), bf16[16,32,128]{2,1,0:T(8,128)(2,1)S(1)}, u32[]{:S(2)}, u32[]{:S(2)}) %all-to-all-start.6) | async-done | bytes 131104 | tf_op jit(solution)/shard_map/all_to_all | solution.py:106
  158.7 1.1 suffix.1
  (10 shorter events, 0.0 us)
Async XLA Ops:
  7.2 85.8 %copy-start.5 = (bf16[256,512]{1,0:T(8,128)(2,1)S(1)}, bf16[256,512]{1,0:T(8,128)(2,1)}, u32[]{:S(2)}) copy-start(bf16[256,512]{1,0:T(8,128)(2,1)} %refs_1_.9) | copy-start | bytes 786436
  7.2 85.8 %copy-start.3 = (bf16[256,512]{1,0:T(8,128)(2,1)S(1)}, bf16[256,512]{1,0:T(8,128)(2,1)}, u32[]{:S(2)}) copy-start(bf16[256,512]{1,0:T(8,128)(2,1)} %refs_0_.7) | copy-start | bytes 786436
  7.2 85.8 %copy-start.6 = (bf16[256,512]{1,0:T(8,128)(2,1)S(1)}, bf16[256,512]{1,0:T(8,128)(2,1)}, u32[]{:S(2)}) copy-start(bf16[256,512]{1,0:T(8,128)(2,1)} %refs_0_.6) | copy-start | bytes 786436
  7.2 96.5 %all-gather.2.cloned.1.call-start = ((), (), s32[]{:S(2)}) async-start(), calls=%async_computation.8 | async-start | bytes 4456448 | tf_op jit(solution)/shard_map/all_gather | solution.py:255
  19.2 1.0 copy-start.2
  20.2 0.9 copy-start.4
  22.1 22.5 %all-to-all-start = ((bf16[16,32,128]{2,1,0:T(8,128)(2,1)}), bf16[16,32,128]{2,1,0:T(8,128)(2,1)S(1)}, u32[]{:S(2)}, u32[]{:S(2)}) async-start(bf16[16,32,128]{2,1,0:T(8,128)(2,1)} %bitcast.2), calls=%async_computation | async-start | bytes 262144 | tf_op jit(solution)/shard_map/all_to_all | solution.py:86
  28.7 12.8 %collective-permute-start.1 = (bf16[256,512]{1,0:T(8,128)(2,1)}, bf16[256,512]{1,0:T(8,128)(2,1)S(1)}, u32[]{:S(2)}, u32[]{:S(2)}) collective-permute-start(bf16[256,512]{1,0:T(8,128)(2,1)} %refs_1_.6), channel_id=1, source_target_pairs={{0,4},{1,5},{2,6},{3,7},{4,0},{5,1},{6,2},{7,3},{8,12},{9,13},{10,... | collective-permute-start | bytes 786440 | tf_op jit(solution)/shard_map/ppermute | solution.py:244
  32.7 11.5 %collective-permute-start = (bf16[256,512]{1,0:T(8,128)(2,1)}, bf16[256,512]{1,0:T(8,128)(2,1)S(1)}, u32[]{:S(2)}, u32[]{:S(2)}) collective-permute-start(bf16[256,512]{1,0:T(8,128)(2,1)} %refs_1_.6), channel_id=1, source_target_pairs={{0,6},{1,7},{2,0},{3,1},{4,2},{5,3},{6,4},{7,5},{8,14},{9,15},{10,... | collective-permute-start | bytes 786440 | tf_op jit(solution)/shard_map/ppermute | solution.py:244
  36.1 8.5 %collective-permute-start.2 = (bf16[256,512]{1,0:T(8,128)(2,1)}, bf16[256,512]{1,0:T(8,128)(2,1)S(1)}, u32[]{:S(2)}, u32[]{:S(2)}) collective-permute-start(bf16[256,512]{1,0:T(8,128)(2,1)} %refs_1_.6), channel_id=1, source_target_pairs={{0,2},{1,3},{2,4},{3,5},{4,6},{5,7},{6,0},{7,1},{8,10},{9,11},{10,... | collective-permute-start | bytes 786440 | tf_op jit(solution)/shard_map/ppermute | solution.py:244
  44.6 1.0 copy-start.9
  46.2 57.5 %copy-start = (bf16[4,256,512]{2,1,0:T(8,128)(2,1)}, bf16[4,256,512]{2,1,0:T(8,128)(2,1)S(1)}, u32[]{:S(2)}) copy-start(bf16[4,256,512]{2,1,0:T(8,128)(2,1)S(1)} %get-tuple-element.17.refs_3_.own_hbm) | copy-start | bytes 3145732
  46.2 28.0 %collective-permute-start.3 = (bf16[4,256,512]{2,1,0:T(8,128)(2,1)S(1)}, bf16[4,256,512]{2,1,0:T(8,128)(2,1)S(1)}, u32[]{:S(2)}, u32[]{:S(2)}) collective-permute-start(bf16[4,256,512]{2,1,0:T(8,128)(2,1)S(1)} %get-tuple-element.17.refs_3_.own_hbm), channel_id=1, source_target_pairs={{0,1},{1,0},{2,3},{3,2},{4,5},{5,4},{6,7},{7,6},{8,9},{9,8},{10,11... | collective-permute-start | bytes 3145736 | tf_op jit(solution)/shard_map/ppermute | solution.py:244
  48.1 26.1 %all-to-all-start.2 = ((bf16[4,32,128]{2,1,0:T(8,128)(2,1)}), bf16[4,32,128]{2,1,0:T(8,128)(2,1)S(1)}, u32[]{:S(2)}, u32[]{:S(2)}) async-start(bf16[4,32,128]{2,1,0:T(8,128)(2,1)} %get-tuple-element.19), calls=%async_computation.2 | async-start | bytes 65536 | tf_op jit(solution)/shard_map/all_to_all | solution.py:95
  74.2 29.5 %copy-start.1 = (bf16[4,256,512]{2,1,0:T(8,128)(2,1)}, bf16[4,256,512]{2,1,0:T(8,128)(2,1)S(1)}, u32[]{:S(2)}) copy-start(bf16[4,256,512]{2,1,0:T(8,128)(2,1)S(1)} %collective-permute-done.3.refs_4_.other_hbm) | copy-start | bytes 3145732
  74.9 18.0 %all-to-all-start.3 = ((bf16[16,32,128]{2,1,0:T(8,128)(2,1)}), bf16[16,32,128]{2,1,0:T(8,128)(2,1)S(1)}, u32[]{:S(2)}, u32[]{:S(2)}) async-start(bf16[16,32,128]{2,1,0:T(8,128)(2,1)} %far_scan.2), calls=%async_computation.3 | async-start | bytes 262144 | tf_op jit(solution)/shard_map/all_to_all | solution.py:106
  81.6 78.2 %reduce-scatter.2.cloned.1.call-start = ((), (), s32[]{:S(2)}) async-start(), calls=%async_computation.9 | async-start | bytes 2359296 | tf_op jit(solution)/shard_map/reduce_scatter | solution.py:267
  93.7 0.9 copy-start.8
  94.5 55.3 %copy-start.7 = (bf16[256,512]{1,0:T(8,128)(2,1)S(1)}, bf16[256,512]{1,0:T(8,128)(2,1)}, u32[]{:S(2)}) copy-start(bf16[256,512]{1,0:T(8,128)(2,1)} %refs_0_.6) | copy-start | bytes 786436
  146.3 12.4 %all-to-all-start.6 = ((bf16[16,32,128]{2,1,0:T(8,128)(2,1)}), bf16[16,32,128]{2,1,0:T(8,128)(2,1)S(1)}, u32[]{:S(2)}, u32[]{:S(2)}) async-start(bf16[16,32,128]{2,1,0:T(8,128)(2,1)} %far_scan.3), calls=%async_computation.7 | async-start | bytes 262144 | tf_op jit(solution)/shard_map/all_to_all | solution.py:106
  149.8 1.0 copy-start.10
Sparse Core Ops, SparseCore 0:
  19.4 84.2 all-gather.1
  111.4 33.2 reduce-scatter.1

commit v3 on v1

v3 whole, which is shorter than its diff:
```python
import jax
import jax.numpy as jnp
from jax import lax
from jax.experimental import pallas as pl
from jax.experimental.pallas import tpu as pltpu
from jax.sharding import Mesh, PartitionSpec as P

HEAD_DIM = 128
NEAR = 16
F32 = jnp.float32
BF16 = jnp.bfloat16
CHUNK = 64
AXES = ("zh", "zl", "y", "x", "core")
SIZES = (4, 4, 4, 4, 2)
PARAMS = pltpu.CompilerParams(vmem_limit_bytes=24 * 1024 * 1024)


def dot(left, right, dims):
    return lax.dot_general(left, right, (dims, ((), ())), preferred_element_type=F32)


def shape_of(dims, dtype):
    return jax.ShapeDtypeStruct(dims, dtype)


def call(kernel, out_shape, *operands, smem=0, after=(), scratch=(), name=None):
    count = len(operands)
    spaces = [pltpu.SMEM] * smem + [pltpu.VMEM] * (count - smem) + [pl.ANY] * len(after)
    operands = operands + tuple(after)

    def body(*refs):
        kernel(*refs[:count], *refs[count + len(after) :])

    return pl.pallas_call(
        body,
        out_shape=out_shape,
        in_specs=[pl.BlockSpec(memory_space=s) for s in spaces],
        scratch_shapes=scratch,
        compiler_params=PARAMS,
        name=name,
    )(*operands)


def head_cols(head):
    return slice(head * HEAD_DIM, (head + 1) * HEAD_DIM)


def causal_mask(length):
    rows = lax.broadcasted_iota(jnp.int32, (length, length), 0)
    cols = lax.broadcasted_iota(jnp.int32, (length, length), 1)
    return rows >= cols


def state_kernel(left_ref, right_ref, out_ref):
    for head in range(left_ref.shape[1] // HEAD_DIM):
        cols = head_cols(head)
        out_ref[cols, :] = dot(left_ref[:, cols], right_ref[:, cols], ((0,), (0,))).astype(BF16)


def near_kernel(reverse, pieces_ref, *refs):
    scan_ref, total_ref = refs[-3:-1] if len(refs) > 2 else refs
    for at, grad_ref in enumerate(refs[:-3]):
        refs[-1][at] = grad_ref[...]
    count = pieces_ref.shape[0]
    running = jnp.zeros(pieces_ref.shape[1:], F32)
    for step in range(count):
        at = count - 1 - step if reverse else step
        scan_ref[at] = running
        running = running + pieces_ref[at].astype(F32)
    total = running.astype(BF16)
    for at in range(total_ref.shape[0]):
        total_ref[at] = total


def far_kernel(reverse, group_ref, scan_ref, totals_ref, out_ref):
    group = group_ref[0]
    offset = jnp.zeros(scan_ref.shape[1:], F32)
    for other in range(totals_ref.shape[0]):
        counts = other > group if reverse else other < group
        offset = offset + jnp.where(counts, totals_ref[other].astype(F32), 0.0)
    for at in range(scan_ref.shape[0]):
        out_ref[at] = (scan_ref[at] + offset).astype(BF16)


def outside_sum(local, group, reverse, grads=(), near_after=None, far_after=None):
    near = ("zl", "y")
    piece = (NEAR, local.shape[0] // NEAR, HEAD_DIM)
    pieces = lax.all_to_all(local.reshape(piece), near, 0, 0, tiled=True)
    stacked = (shape_of((len(grads),) + grads[0].shape, BF16),) if grads else ()
    scan, total, *stack = call(
        lambda *refs: near_kernel(reverse, *refs),
        (shape_of(piece, F32), shape_of((SIZES[0],) + piece[1:], BF16)) + stacked,
        pieces, *grads,
        after=near_after() if near_after else (),
        name="near_scan",
    )
    totals = lax.all_to_all(total, "zh", 0, 0, tiled=True)
    stack += [permute(own, half=1) for own in stack]
    sums = call(
        lambda *refs: far_kernel(reverse, *refs),
        shape_of(piece, BF16),
        group,
        scan,
        totals,
        smem=1,
        after=far_after(*stack) if far_after else (),
        name="far_scan",
    )
    return lax.all_to_all(sums, near, 0, 0, tiled=True).reshape(local.shape), *stack


def pack_kernel(grad_ref, out_ref):
    half = grad_ref.shape[1] // 2
    for y in range(out_ref.shape[0]):
        low = slice(y * CHUNK, (y + 1) * CHUNK)
        high = slice(half + y * CHUNK, half + (y + 1) * CHUNK)
        out_ref[y] = jnp.concatenate([grad_ref[:, low], grad_ref[:, high]], axis=1)


def unpack_kernel(place_ref, part0_ref, part1_ref, part2_ref, part3_ref, out_ref, slots_ref):
    parts = (part0_ref, part1_ref, part2_ref, part3_ref)
    for back, part_ref in enumerate(parts):
        slots_ref[lax.rem(place_ref[2] + 4 - back, 4)] = part_ref[...]
    pieces = [slots_ref[y][:, half * CHUNK : (half + 1) * CHUNK] for half in range(2) for y in range(4)]
    for pair in range(4):
        cols = head_cols(pair)
        out_ref[:, cols] = jnp.concatenate(pieces[2 * pair : 2 * pair + 2], axis=1)


def forward_kernel(query_ref, key_ref, value_ref, prefix_ref, numer_ref, attended_ref):
    causal = causal_mask(query_ref.shape[0])
    for head in range(query_ref.shape[1] // HEAD_DIM):
        cols = head_cols(head)
        query = query_ref[:, cols]
        scores = dot(query, key_ref[:, cols], ((1,), (1,)))
        weights = jnp.where(causal, scores, 0.0).astype(BF16)
        numer = dot(weights, value_ref[:, cols], ((1,), (0,)))
        numer = numer + dot(query, prefix_ref[cols, :], ((1,), (0,)))
        spread = jnp.sqrt(jnp.mean(numer * numer, axis=-1, keepdims=True) + 1e-06)
        numer_ref[:, cols] = numer
        attended_ref[:, cols] = (numer / spread).astype(BF16)


def partial_kernel(
    place_ref, own_hbm, other_hbm, weight0_hbm, ahead1_hbm, back1_hbm, ahead2_hbm, back2_hbm,
    out0_ref, out1_ref, out2_ref, out3_ref, weight_ref, grad_ref, sems,
):
    across, core, y, near = (place_ref[at] for at in range(4))
    rows = out0_ref.shape[0]

    def at_class(ahead):
        return lax.rem(near + ahead, 4)

    def half_of(owner):
        return pl.ds(pl.multiple_of(owner * HEAD_DIM, HEAD_DIM), HEAD_DIM)

    copies = [
        pltpu.make_async_copy(source, target, sems.at[at])
        for at, (source, target) in enumerate((
            (own_hbm, grad_ref.at[:, :, half_of(core)]),
            (other_hbm, grad_ref.at[:, :, half_of(1 - core)]),
            (weight0_hbm, weight_ref.at[:, at_class(0)]),
            (ahead1_hbm, weight_ref.at[:, at_class(1)]),
            (back1_hbm, weight_ref.at[:, at_class(3)]),
            (ahead2_hbm, weight_ref.at[pl.ds(0, 2), at_class(2)]),
            (back2_hbm, weight_ref.at[pl.ds(2, 2), at_class(2)]),
        ))
    ]
    for copy in copies:
        copy.start()
    for copy in copies:
        copy.wait()
    weights = [weight_ref[lax.rem(across + ahead, 4)].reshape(4 * CHUNK, -1) for ahead in range(4)]
    for block, out_ref in enumerate((out0_ref, out1_ref, out2_ref, out3_ref)):
        tokens = pl.ds(pl.multiple_of(lax.rem(y + block, 4) * rows, rows), rows)
        total = dot(grad_ref[0, tokens, :], weights[0], ((1,), (0,)))
        for ahead in range(1, 4):
            total = total + dot(grad_ref[ahead, tokens, :], weights[ahead], ((1,), (0,)))
        out_ref[...] = total


def partial_out_grad(place, own, other, weights, rows):
    width = weights[0].shape[-1]
    vmem = pl.BlockSpec(memory_space=pltpu.VMEM)
    hbm = pl.BlockSpec(memory_space=pl.ANY)
    return pl.pallas_call(
        partial_kernel,
        out_shape=(shape_of((rows, width), F32),) * 4 + (shape_of((4, 4, CHUNK, width), BF16),),
        in_specs=[pl.BlockSpec(memory_space=pltpu.SMEM)] + [hbm] * 7,
        out_specs=[vmem] * 5,
        scratch_shapes=[pltpu.VMEM((4, 4 * rows, 2 * HEAD_DIM), BF16), pltpu.SemaphoreType.DMA((7,))],
        compiler_params=PARAMS,
        name="partial",
    )(place, own, other, *weights)


def middle_kernel(part0_ref, part1_ref, part2_ref, part3_ref, query_ref, numer_ref, numer_grad_ref, local_grad_ref):
    for head in range(query_ref.shape[1] // HEAD_DIM):
        cols = head_cols(head)
        numer = numer_ref[:, cols]
        spread = jnp.sqrt(jnp.mean(numer * numer, axis=-1, keepdims=True) + 1e-06)
        normed = numer / spread
        direction = part0_ref[:, cols] + part1_ref[:, cols] + part2_ref[:, cols] + part3_ref[:, cols]
        along = jnp.mean(direction * normed, axis=-1, keepdims=True)
        numer_grad = ((direction - normed * along) / spread).astype(BF16)
        numer_grad_ref[:, cols] = numer_grad
        local_grad_ref[cols, :] = dot(query_ref[:, cols], numer_grad, ((0,), (0,))).astype(BF16)


def mixed_kernel(place_ref, att0_ref, att1_ref, att2_ref, att3_ref, weight_ref, own_ref, other_ref):
    across, core, y = (place_ref[at] for at in range(3))
    for chip in range(4):
        weight = weight_ref[lax.rem(across + chip, 4)].reshape(4 * CHUNK, -1)
        for ahead, att_ref in enumerate((att0_ref, att1_ref, att2_ref, att3_ref)):
            block = dot(att_ref[...], weight, ((1,), (1,)))
            low, high = block[:, :HEAD_DIM], block[:, HEAD_DIM:]
            at = lax.rem(y + ahead, 4)
            own_ref[chip, at] = jnp.where(core == 0, low, high).astype(BF16)
            other_ref[chip, at] = jnp.where(core == 0, high, low).astype(BF16)


def core_sum_kernel(own_ref, other_ref, *out_refs):
    for chip, out_ref in enumerate(out_refs):
        for y in range(out_ref.shape[0]):
            out_ref[y] = (own_ref[chip, y].astype(F32) + other_ref[chip, y].astype(F32)).astype(BF16)


def chip_sum_kernel(place_ref, sum0_ref, sum1_ref, sum2_ref, sum3_ref, *out_refs):
    for ahead, out_ref in enumerate(out_refs):
        at = lax.rem(place_ref[2] + ahead, 4)
        total = sum0_ref[at].astype(F32) + sum1_ref[at].astype(F32)
        out_ref[...] = (total + sum2_ref[at].astype(F32) + sum3_ref[at].astype(F32)).astype(BF16)


def backward_kernel(
    query_ref, key_ref, value_ref, numer_grad_ref, prefix_ref, query_out, key_part, value_part
):
    causal = causal_mask(query_ref.shape[0])
    for head in range(query_ref.shape[1] // HEAD_DIM):
        cols = head_cols(head)
        query, key, value = query_ref[:, cols], key_ref[:, cols], value_ref[:, cols]
        numer_grad = numer_grad_ref[:, cols]
        weights = jnp.where(causal, dot(query, key, ((1,), (1,))), 0.0).astype(BF16)
        pairs = jnp.where(causal, dot(numer_grad, value, ((1,), (1,))), 0.0).astype(BF16)
        query_out[:, cols] = (
            dot(pairs, key, ((1,), (0,))) + dot(numer_grad, prefix_ref[cols, :], ((1,), (1,)))
        ).astype(BF16)
        key_part[:, cols] = dot(pairs, query, ((0,), (0,)))
        value_part[:, cols] = dot(weights, numer_grad, ((0,), (0,)))


def suffix_kernel(key_ref, value_ref, suffix_ref, key_part, value_part, key_out, value_out):
    for head in range(key_ref.shape[1] // HEAD_DIM):
        cols = head_cols(head)
        suffix = suffix_ref[cols, :]
        key_out[:, cols] = (key_part[:, cols] + dot(value_ref[:, cols], suffix, ((1,), (1,)))).astype(BF16)
        value_out[:, cols] = (value_part[:, cols] + dot(key_ref[:, cols], suffix, ((1,), (0,)))).astype(BF16)


def permute(value, z=0, y=0, x=0, half=0):
    along_zh, along_zl, along_y, along_x, cores = SIZES
    along_z = along_zh * along_zl

    def number(at_z, at_y, at_x, at_core):
        return (((at_z % along_z) * along_y + at_y % along_y) * along_x + at_x % along_x) * cores + at_core

    pairs = [
        (number(at_z + z, at_y + y, at_x + x, at_core ^ half), number(at_z, at_y, at_x, at_core))
        for at_z in range(along_z)
        for at_y in range(along_y)
        for at_x in range(along_x)
        for at_core in range(cores)
    ]
    return lax.ppermute(value, AXES, pairs)


def per_device(queries, key_rows, values, out_weight, out_grad):
    rows, width = queries.shape
    group = lax.axis_index("zh").astype(jnp.int32).reshape(1)
    place = jnp.stack([lax.axis_index(name) for name in ("x", "core", "y", "zl")]).astype(jnp.int32)

    weight = out_weight.T
    copies = jnp.broadcast_to(weight[None], (SIZES[0],) + weight.shape)
    weight = lax.all_to_all(copies, "zh", 0, 0, tiled=True)
    weights = (
        weight, permute(weight, z=1), permute(weight, z=-1), permute(weight[:2], z=2), permute(weight[2:], z=-2)
    )

    packed = call(pack_kernel, shape_of((SIZES[2], rows, HEAD_DIM), BF16), out_grad, name="pack")
    grad = lax.all_to_all(packed, "y", 0, 0, tiled=True).reshape(SIZES[2] * rows, HEAD_DIM)
    grads = [grad] + [permute(grad, x=ahead) for ahead in (1, 2, 3)]

    local_state = call(
        state_kernel, shape_of((width, HEAD_DIM), BF16), key_rows, values, after=(weight, *grads[1:]), name="state"
    )
    parts = []

    def start_parts(own, other):
        parts.extend(partial_out_grad(place, own, other, weights, rows))
        return parts[-1:]

    prefix, *_ = outside_sum(local_state, group, False, grads, lambda: weights[1:], start_parts)
    *parts, weight = parts
    parts = [parts[0]] + [permute(parts[ahead], y=-ahead) for ahead in (1, 2, 3)]
    numer, attended = call(
        forward_kernel,
        (shape_of((rows, width), F32), shape_of((rows, width), BF16)),
        queries, key_rows, values, prefix,
        after=parts,
        name="forward",
    )
    blocks = [attended] + [permute(attended, y=ahead) for ahead in (1, 2, 3)]
    numer_grad, local_grad = call(
        middle_kernel,
        (shape_of((rows, width), BF16), shape_of((width, HEAD_DIM), BF16)),
        *parts, queries, numer,
        name="middle",
    )

    shares = shape_of((4, 4, rows, HEAD_DIM), BF16)
    own, other = call(mixed_kernel, (shares, shares), place, *blocks, weight, smem=1, after=(local_grad,), name="mixed")
    other = permute(other, half=1)
    sums = call(core_sum_kernel, (shape_of((4, rows, HEAD_DIM), BF16),) * 4, own, other, name="core_sum")
    sums = [sums[0]] + [permute(sums[ahead], x=-ahead) for ahead in (1, 2, 3)]
    tokens = call(
        chip_sum_kernel, (shape_of((rows, HEAD_DIM), BF16),) * 4, place, *sums, smem=1, name="chip_sum"
    )
    tokens = [tokens[0]] + [permute(tokens[ahead], y=-ahead) for ahead in (1, 2, 3)]
    mixed = call(
        unpack_kernel,
        shape_of((rows, width), BF16),
        place, *tokens,
        smem=1,
        scratch=[pltpu.VMEM((4, rows, HEAD_DIM), BF16)],
        name="unpack",
    )

    (suffix,) = outside_sum(
        local_grad, group, True, near_after=lambda: (other,), far_after=lambda: tuple(sums[1:])
    )
    query_out, key_part, value_part = call(
        backward_kernel,
        (shape_of((rows, width), BF16),) + (shape_of((rows, width), F32),) * 2,
        queries, key_rows, values, numer_grad, prefix,
        name="backward",
    )
    key_out, value_out = call(
        suffix_kernel,
        (shape_of((rows, width), BF16),) * 2,
        key_rows, values, suffix, key_part, value_part,
        name="suffix",
    )
    return mixed, query_out, key_out, value_out


def solution(mesh):
    fine = Mesh(mesh.devices.reshape(SIZES), AXES)
    seq, head = ("zh", "zl", "y"), ("x", "core")
    rows = P(seq, head)
    return jax.shard_map(
        per_device,
        mesh=fine,
        in_specs=(rows, rows, rows, P(head, seq), rows),
        out_specs=(rows, rows, rows, rows),
        check_vma=False,
    )
```

time: 169 us -> 227 us (1.34)
  the two profiles are of different devices: /device:TPU:2 before, /device:TPU:24 now
where the time goes in v3:
time: 227 us; the launch traced here: 226 us
  starting transfers between devices  112 us (49%)
  blocking collectives  59.4 us (26%)
  waiting for transfers between devices  21 us (9%)
  Pallas kernels  18.5 us (8%)
  local copies, waits for them, and re-layouts  13.9 us (6%)
    ppermute x21, starting transfers between devices, permute(): return lax.ppermute(value, AXES, pairs)  69.1 us
    all_to_all x1, blocking collectives, outside_sum(): totals = lax.all_to_all(total, 'zh', 0, 0, tiled=True)  24.6 us
    all_to_all x1, blocking collectives, outside_sum(): lax.all_to_all(sums, near, 0, 0, tiled=True).reshape(local.shape)  22.1 us
    ppermute x21, waiting for transfers between devices, permute(): return lax.ppermute(value, AXES, pairs)  21 us
    pallas_call x14, Pallas kernels, call(): pl.pallas_call(body, out_shape=out_shape, in_specs=[pl.BlockSpec(memory_s...  15.1 us
    all_to_all x2, starting transfers between devices, outside_sum(): pieces = lax.all_to_all(local.reshape(piece), near, 0, 0, tiled=True)  13.9 us
    unnamed x50, local copies, waits for them, and re-layouts  13.2 us
    all_to_all x1, blocking collectives, per_device(): lax.all_to_all(packed, 'y', 0, 0, tiled=True)  12.7 us
  transfers between devices with their start and end apart: 26, of which 7 were waited for; matrix products, arithmetic and copies ran while one was open for 0% of the time, Pallas kernels for 5%

profile of v3, /device:TPU:24, one launch (start us, length us, event | category | flops | bytes accessed | tf_op | source)
XLA Modules:
  0.0 225.7 jit_solution(7783593530360162076)
XLA Ops:
  1.7 12.7 %all_to_all.40 = bf16[4,256,128]{2,1,0:T(8,128)(2,1)S(1)} all-to-all(bf16[4,256,128]{2,1,0:T(8,128)(2,1)S(1)} %pack.1), channel_id=1, replica_groups=mesh['zh'=4,'zl'=4,'y'=4,'x'=4,'core'=2] {'y'}, dimensions={0} | all-to-all | bytes 524288 | tf_op jit(solution)/shard_map/all_to_all | solution.py:290
  15.2 11.7 %all-to-all-start = ((bf16[4,64,512]{2,1,0:T(8,128)(2,1)}), bf16[4,64,512]{2,1,0:T(8,128)(2,1)S(1)}, u32[]{:S(2)}, u32[]{:S(2)}) async-start(bf16[4,64,512]{2,1,0:T(8,128)(2,1)} %broadcast_in_dim.2), calls=%async_computation | async-start | bytes 524288 | tf_op jit(solution)/shard_map/all_to_all | solution.py:284
  26.9 3.4 %collective-permute-start.2 = (bf16[1024,128]{1,0:T(8,128)(2,1)S(1)}, bf16[1024,128]{1,0:T(8,128)(2,1)S(1)}, u32[]{:S(2)}, u32[]{:S(2)}) collective-permute-start(bf16[1024,128]{1,0:T(8,128)(2,1)S(1)} %bitcast.13), channel_id=1, source_target_pairs={{6,0},{7,1},{0,2},{1,3},{2,4},{3,5},{4,6},{5,7},{14,8},{15,9},{8,1... | collective-permute-start | bytes 786440 | tf_op jit(solution)/shard_map/ppermute | solution.py:274
  30.3 4.6 %collective-permute-start.1 = (bf16[1024,128]{1,0:T(8,128)(2,1)S(1)}, bf16[1024,128]{1,0:T(8,128)(2,1)S(1)}, u32[]{:S(2)}, u32[]{:S(2)}) collective-permute-start(bf16[1024,128]{1,0:T(8,128)(2,1)S(1)} %bitcast.14), channel_id=1, source_target_pairs={{4,0},{5,1},{6,2},{7,3},{0,4},{1,5},{2,6},{3,7},{12,8},{13,9},{14,... | collective-permute-start | bytes 786440 | tf_op jit(solution)/shard_map/ppermute | solution.py:274
  35.0 3.3 %collective-permute-start = (bf16[1024,128]{1,0:T(8,128)(2,1)S(1)}, bf16[1024,128]{1,0:T(8,128)(2,1)S(1)}, u32[]{:S(2)}, u32[]{:S(2)}) collective-permute-start(bf16[1024,128]{1,0:T(8,128)(2,1)S(1)} %bitcast.15), channel_id=1, source_target_pairs={{2,0},{3,1},{4,2},{5,3},{6,4},{7,5},{0,6},{1,7},{10,8},{11,9},{12,... | collective-permute-start | bytes 786440 | tf_op jit(solution)/shard_map/ppermute | solution.py:274
  38.3 4.6 %collective-permute-done.1.refs_4_.refs_3_ = bf16[1024,128]{1,0:T(8,128)(2,1)S(1)} collective-permute-done((bf16[1024,128]{1,0:T(8,128)(2,1)S(1)}, bf16[1024,128]{1,0:T(8,128)(2,1)S(1)}, u32[]{:S(2)}, u32[]{:S(2)}) %collective-permute-start.1) | collective-permute-done | bytes 262176 | tf_op jit(solution)/shard_map/ppermute | solution.py:274
  42.9 1.8 collective-permute-done.refs_3_.refs_2_
  45.7 7.2 %all-to-all-start.2 = ((bf16[16,32,128]{2,1,0:T(8,128)(2,1)}), bf16[16,32,128]{2,1,0:T(8,128)(2,1)S(1)}, u32[]{:S(2)}, u32[]{:S(2)}) async-start(bf16[16,32,128]{2,1,0:T(8,128)(2,1)} %bitcast.7), calls=%async_computation.2 | async-start | bytes 262144 | tf_op jit(solution)/shard_map/all_to_all | solution.py:88
  53.0 3.4 %collective-permute-start.4 = (bf16[4,64,512]{2,1,0:T(8,128)(2,1)S(1)}, bf16[4,64,512]{2,1,0:T(8,128)(2,1)S(1)}, u32[]{:S(2)}, u32[]{:S(2)}) collective-permute-start(bf16[4,64,512]{2,1,0:T(8,128)(2,1)S(1)} %all-to-all-done.refs_2_.weight0_hbm), channel_id=1, source_target_pairs={{480,0},{481,1},{482,2},{483,3},{484,4},{485,5},{486,6},{487,7},{4... | collective-permute-start | bytes 786440 | tf_op jit(solution)/shard_map/ppermute | solution.py:274
  56.3 5.0 %collective-permute-start.3 = (bf16[4,64,512]{2,1,0:T(8,128)(2,1)S(1)}, bf16[4,64,512]{2,1,0:T(8,128)(2,1)S(1)}, u32[]{:S(2)}, u32[]{:S(2)}) collective-permute-start(bf16[4,64,512]{2,1,0:T(8,128)(2,1)S(1)} %all-to-all-done.refs_2_.weight0_hbm), channel_id=1, source_target_pairs={{32,0},{33,1},{34,2},{35,3},{36,4},{37,5},{38,6},{39,7},{40,8},{41... | collective-permute-start | bytes 786440 | tf_op jit(solution)/shard_map/ppermute | solution.py:274
  61.4 1.9 collective-permute-start.6
  63.3 6.0 %collective-permute-start.5 = (bf16[2,64,512]{2,1,0:T(8,128)(2,1)S(1)}, bf16[2,64,512]{2,1,0:T(8,128)(2,1)S(1)}, u32[]{:S(2)}, u32[]{:S(2)}) collective-permute-start(bf16[2,64,512]{2,1,0:T(8,128)(2,1)S(1)} %get-tuple-element.63), channel_id=1, source_target_pairs={{64,0},{65,1},{66,2},{67,3},{68,4},{69,5},{70,6},{71,7},{72,8},{73... | collective-permute-start | bytes 393224 | tf_op jit(solution)/shard_map/ppermute | solution.py:274
  69.4 2.1 collective-permute-done.6.refs_8_.back2_hbm
  72.1 1.1 collective-permute-done.5.refs_7_.ahead2_hbm
  73.9 1.1 copy-done.11
  77.3 1.9 collective-permute-start.7
  79.2 9.8 %all-to-all-start.3 = ((bf16[4,32,128]{2,1,0:T(8,128)(2,1)}), bf16[4,32,128]{2,1,0:T(8,128)(2,1)}, u32[]{:S(2)}, u32[]{:S(2)}) async-start(bf16[4,32,128]{2,1,0:T(8,128)(2,1)} %copy-done.23), calls=%async_computation.3 | async-start | bytes 65536 | tf_op jit(solution)/shard_map/all_to_all | solution.py:97
  89.1 1.0 copy-done.3
  90.1 1.2 copy-done.4
  91.3 0.9 copy-done.6
  92.3 0.9 copy-done.8
  95.0 3.4 %partial.1 = (f32[256,512]{1,0:T(8,128)S(1)}, f32[256,512]{1,0:T(8,128)}, f32[256,512]{1,0:T(8,128)}, f32[256,512]{1,0:T(8,128)}, bf16[4,4,64,512]{3,2,1,0:T(8,128)(2,1)S(1)}) custom-call(s32[4]{0:T(128)S(1)} %pad_add_fusion.place_ref.refs_0_, bf16[4,1024,128]{2,1,0:T(8,128)(2,1)S(1)} %get-tuple-element.35.own_hbm, bf16[4,1024,128]{2,1,0:T(8,128)(2,1)S(1)} %copy-done.4, ...), custom_call_target="tpu_custom_call" | custom-call | tf_op jit(solution)/shard_map/partial/pallas_call | solution.py:186
  98.4 2.5 %collective-permute-start.8 = (f32[256,512]{1,0:T(8,128)}, f32[256,512]{1,0:T(8,128)S(1)}, u32[]{:S(2)}, u32[]{:S(2)}) collective-permute-start(f32[256,512]{1,0:T(8,128)} %get-tuple-element.38), channel_id=1, source_target_pairs={{24,0},{25,1},{26,2},{27,3},{28,4},{29,5},{30,6},{31,7},{0,8},{1,9... | collective-permute-start | bytes 1572872 | tf_op jit(solution)/shard_map/ppermute | solution.py:274
  100.9 4.3 %collective-permute-start.9 = (f32[256,512]{1,0:T(8,128)}, f32[256,512]{1,0:T(8,128)S(1)}, u32[]{:S(2)}, u32[]{:S(2)}) collective-permute-start(f32[256,512]{1,0:T(8,128)} %get-tuple-element.39), channel_id=1, source_target_pairs={{16,0},{17,1},{18,2},{19,3},{20,4},{21,5},{22,6},{23,7},{24,8},{25... | collective-permute-start | bytes 1572872 | tf_op jit(solution)/shard_map/ppermute | solution.py:274
  105.2 1.9 collective-permute-start.10
  108.9 22.1 %all_to_all.41 = bf16[16,32,128]{2,1,0:T(8,128)(2,1)S(1)} all-to-all(bf16[16,32,128]{2,1,0:T(8,128)(2,1)S(1)} %far_scan.2), channel_id=1, replica_groups=mesh['zh'=4,'zl'=4,'y'=4,'x'=4,'core'=2] {'zl','y'}, dimensions={0} | all-to-all | bytes 262144 | tf_op jit(solution)/shard_map/all_to_all | solution.py:109
  131.7 2.4 %collective-permute-start.13 = (bf16[256,512]{1,0:T(8,128)(2,1)S(1)}, bf16[256,512]{1,0:T(8,128)(2,1)S(1)}, u32[]{:S(2)}, u32[]{:S(2)}) collective-permute-start(bf16[256,512]{1,0:T(8,128)(2,1)S(1)} %get-tuple-element.41.refs_1_), channel_id=1, source_target_pairs={{24,0},{25,1},{26,2},{27,3},{28,4},{29,5},{30,6},{31,7},{0,8},{1,9... | collective-permute-start | bytes 786440 | tf_op jit(solution)/shard_map/ppermute | solution.py:274
  134.2 4.3 %collective-permute-start.12 = (bf16[256,512]{1,0:T(8,128)(2,1)S(1)}, bf16[256,512]{1,0:T(8,128)(2,1)S(1)}, u32[]{:S(2)}, u32[]{:S(2)}) collective-permute-start(bf16[256,512]{1,0:T(8,128)(2,1)S(1)} %get-tuple-element.41.refs_1_), channel_id=1, source_target_pairs={{16,0},{17,1},{18,2},{19,3},{20,4},{21,5},{22,6},{23,7},{24,8},{25... | collective-permute-start | bytes 786440 | tf_op jit(solution)/shard_map/ppermute | solution.py:274
  138.5 2.7 %collective-permute-start.11 = (bf16[256,512]{1,0:T(8,128)(2,1)S(1)}, bf16[256,512]{1,0:T(8,128)(2,1)S(1)}, u32[]{:S(2)}, u32[]{:S(2)}) collective-permute-start(bf16[256,512]{1,0:T(8,128)(2,1)S(1)} %get-tuple-element.41.refs_1_), channel_id=1, source_target_pairs={{8,0},{9,1},{10,2},{11,3},{12,4},{13,5},{14,6},{15,7},{16,8},{17,9... | collective-permute-start | bytes 786440 | tf_op jit(solution)/shard_map/ppermute | solution.py:274
  141.2 1.7 middle.1
  143.0 3.8 %collective-permute-done.12.refs_3_ = bf16[256,512]{1,0:T(8,128)(2,1)S(1)} collective-permute-done((bf16[256,512]{1,0:T(8,128)(2,1)S(1)}, bf16[256,512]{1,0:T(8,128)(2,1)S(1)}, u32[]{:S(2)}, u32[]{:S(2)}) %collective-permute-start.12) | collective-permute-done | bytes 262176 | tf_op jit(solution)/shard_map/ppermute | solution.py:274
  146.8 4.1 %collective-permute-done.11.refs_2_ = bf16[256,512]{1,0:T(8,128)(2,1)S(1)} collective-permute-done((bf16[256,512]{1,0:T(8,128)(2,1)S(1)}, bf16[256,512]{1,0:T(8,128)(2,1)S(1)}, u32[]{:S(2)}, u32[]{:S(2)}) %collective-permute-start.11) | collective-permute-done | bytes 262176 | tf_op jit(solution)/shard_map/ppermute | solution.py:274
  150.9 2.9 %mixed.1 = (bf16[4,4,256,128]{3,2,1,0:T(8,128)(2,1)S(1)}, bf16[4,4,256,128]{3,2,1,0:T(8,128)(2,1)}) custom-call(s32[4]{0:T(128)S(1)} %pad_add_fusion.place_ref.refs_0_, bf16[256,512]{1,0:T(8,128)(2,1)S(1)} %get-tuple-element.41.refs_1_, bf16[256,512]{1,0:T(8,128)(2,1)S(1)} %collective-permute-done.11.refs_2_, ...), custom_call_target="tpu_custom_call" | custom-call | tf_op jit(solution)/shard_map/mixed/pallas_call | solution.py:34
  153.8 1.9 collective-permute-start.14
  155.7 6.7 %all-to-all-start.5 = ((bf16[16,32,128]{2,1,0:T(8,128)(2,1)}), bf16[16,32,128]{2,1,0:T(8,128)(2,1)}, u32[]{:S(2)}, u32[]{:S(2)}) async-start(bf16[16,32,128]{2,1,0:T(8,128)(2,1)} %bitcast.17), calls=%async_computation.5 | async-start | bytes 262144 | tf_op jit(solution)/shard_map/all_to_all | solution.py:88
  162.4 1.0 core_sum.1
  164.1 3.6 %collective-permute-start.15 = (bf16[4,256,128]{2,1,0:T(8,128)(2,1)}, bf16[4,256,128]{2,1,0:T(8,128)(2,1)S(1)}, u32[]{:S(2)}, u32[]{:S(2)}) collective-permute-start(bf16[4,256,128]{2,1,0:T(8,128)(2,1)} %get-tuple-element.47), channel_id=1, source_target_pairs={{6,0},{7,1},{0,2},{1,3},{2,4},{3,5},{4,6},{5,7},{14,8},{15,9},{8,1... | collective-permute-start | bytes 786440 | tf_op jit(solution)/shard_map/ppermute | solution.py:274
  167.8 4.3 %collective-permute-start.16 = (bf16[4,256,128]{2,1,0:T(8,128)(2,1)}, bf16[4,256,128]{2,1,0:T(8,128)(2,1)S(1)}, u32[]{:S(2)}, u32[]{:S(2)}) collective-permute-start(bf16[4,256,128]{2,1,0:T(8,128)(2,1)} %get-tuple-element.48), channel_id=1, source_target_pairs={{4,0},{5,1},{6,2},{7,3},{0,4},{1,5},{2,6},{3,7},{12,8},{13,9},{14,... | collective-permute-start | bytes 786440 | tf_op jit(solution)/shard_map/ppermute | solution.py:274
  172.1 2.8 %collective-permute-start.17 = (bf16[4,256,128]{2,1,0:T(8,128)(2,1)}, bf16[4,256,128]{2,1,0:T(8,128)(2,1)S(1)}, u32[]{:S(2)}, u32[]{:S(2)}) collective-permute-start(bf16[4,256,128]{2,1,0:T(8,128)(2,1)} %get-tuple-element.49), channel_id=1, source_target_pairs={{2,0},{3,1},{4,2},{5,3},{6,4},{7,5},{0,6},{1,7},{10,8},{11,9},{12,... | collective-permute-start | bytes 786440 | tf_op jit(solution)/shard_map/ppermute | solution.py:274
  175.9 24.6 %all_to_all.42.refs_2_ = bf16[4,32,128]{2,1,0:T(8,128)(2,1)S(1)} all-to-all(bf16[4,32,128]{2,1,0:T(8,128)(2,1)S(1)} %get-tuple-element.57), channel_id=1, replica_groups=mesh['zh'=4,'zl'=4,'y'=4,'x'=4,'core'=2] {'zh'}, dimensions={0} | all-to-all | bytes 65536 | tf_op jit(solution)/shard_map/all_to_all | solution.py:97
  201.2 7.2 %all-to-all-start.7 = ((bf16[16,32,128]{2,1,0:T(8,128)(2,1)}), bf16[16,32,128]{2,1,0:T(8,128)(2,1)S(1)}, u32[]{:S(2)}, u32[]{:S(2)}) async-start(bf16[16,32,128]{2,1,0:T(8,128)(2,1)} %far_scan.3), calls=%async_computation.7 | async-start | bytes 262144 | tf_op jit(solution)/shard_map/all_to_all | solution.py:109
  209.1 2.0 collective-permute-start.18
  211.1 4.7 %collective-permute-start.19 = (bf16[256,128]{1,0:T(8,128)(2,1)S(1)}, bf16[256,128]{1,0:T(8,128)(2,1)S(1)}, u32[]{:S(2)}, u32[]{:S(2)}) collective-permute-start(bf16[256,128]{1,0:T(8,128)(2,1)S(1)} %get-tuple-element.52), channel_id=1, source_target_pairs={{16,0},{17,1},{18,2},{19,3},{20,4},{21,5},{22,6},{23,7},{24,8},{25... | collective-permute-start | bytes 196616 | tf_op jit(solution)/shard_map/ppermute | solution.py:274
  215.9 1.9 collective-permute-start.20
  217.8 2.0 backward.1
  219.8 3.4 %collective-permute-done.20.refs_4_ = bf16[256,128]{1,0:T(8,128)(2,1)S(1)} collective-permute-done((bf16[256,128]{1,0:T(8,128)(2,1)S(1)}, bf16[256,128]{1,0:T(8,128)(2,1)S(1)}, u32[]{:S(2)}, u32[]{:S(2)}) %collective-permute-start.20) | collective-permute-done | bytes 65568 | tf_op jit(solution)/shard_map/ppermute | solution.py:274
  223.3 1.4 unpack.1
  224.7 1.1 suffix.1
  (75 shorter events, 13.9 us)
Async XLA Ops:
  0.6 1.0 copy-start.16
  1.7 12.7 %copy-start.24 = (bf16[512,64]{0,1:T(8,128)(2,1)S(1)}, bf16[512,64]{0,1:T(8,128)(2,1)}, u32[]{:S(2)}) copy-start(bf16[512,64]{0,1:T(8,128)(2,1)} %param.8) | copy-start | bytes 196612
  15.2 29.6 %copy-start = (bf16[256,512]{1,0:T(8,128)(2,1)S(1)}, bf16[256,512]{1,0:T(8,128)(2,1)}, u32[]{:S(2)}) copy-start(bf16[256,512]{1,0:T(8,128)(2,1)} %refs_0_.9) | copy-start | bytes 786436
  15.2 29.6 %copy-start.1 = (bf16[256,512]{1,0:T(8,128)(2,1)S(1)}, bf16[256,512]{1,0:T(8,128)(2,1)}, u32[]{:S(2)}) copy-start(bf16[256,512]{1,0:T(8,128)(2,1)} %refs_1_.7) | copy-start | bytes 786436
  15.2 29.6 %all-to-all-start = ((bf16[4,64,512]{2,1,0:T(8,128)(2,1)}), bf16[4,64,512]{2,1,0:T(8,128)(2,1)S(1)}, u32[]{:S(2)}, u32[]{:S(2)}) async-start(bf16[4,64,512]{2,1,0:T(8,128)(2,1)} %broadcast_in_dim.2), calls=%async_computation | async-start | bytes 524288 | tf_op jit(solution)/shard_map/all_to_all | solution.py:284
  26.9 11.4 %collective-permute-start.2 = (bf16[1024,128]{1,0:T(8,128)(2,1)S(1)}, bf16[1024,128]{1,0:T(8,128)(2,1)S(1)}, u32[]{:S(2)}, u32[]{:S(2)}) collective-permute-start(bf16[1024,128]{1,0:T(8,128)(2,1)S(1)} %bitcast.13), channel_id=1, source_target_pairs={{6,0},{7,1},{0,2},{1,3},{2,4},{3,5},{4,6},{5,7},{14,8},{15,9},{8,1... | collective-permute-start | bytes 786440 | tf_op jit(solution)/shard_map/ppermute | solution.py:274
  30.3 12.6 %collective-permute-start.1 = (bf16[1024,128]{1,0:T(8,128)(2,1)S(1)}, bf16[1024,128]{1,0:T(8,128)(2,1)S(1)}, u32[]{:S(2)}, u32[]{:S(2)}) collective-permute-start(bf16[1024,128]{1,0:T(8,128)(2,1)S(1)} %bitcast.14), channel_id=1, source_target_pairs={{4,0},{5,1},{6,2},{7,3},{0,4},{1,5},{2,6},{3,7},{12,8},{13,9},{14,... | collective-permute-start | bytes 786440 | tf_op jit(solution)/shard_map/ppermute | solution.py:274
  35.0 9.8 %collective-permute-start = (bf16[1024,128]{1,0:T(8,128)(2,1)S(1)}, bf16[1024,128]{1,0:T(8,128)(2,1)S(1)}, u32[]{:S(2)}, u32[]{:S(2)}) collective-permute-start(bf16[1024,128]{1,0:T(8,128)(2,1)S(1)} %bitcast.15), channel_id=1, source_target_pairs={{2,0},{3,1},{4,2},{5,3},{6,4},{7,5},{0,6},{1,7},{10,8},{11,9},{12,... | collective-permute-start | bytes 786440 | tf_op jit(solution)/shard_map/ppermute | solution.py:274
  45.7 28.2 %all-to-all-start.2 = ((bf16[16,32,128]{2,1,0:T(8,128)(2,1)}), bf16[16,32,128]{2,1,0:T(8,128)(2,1)S(1)}, u32[]{:S(2)}, u32[]{:S(2)}) async-start(bf16[16,32,128]{2,1,0:T(8,128)(2,1)} %bitcast.7), calls=%async_computation.2 | async-start | bytes 262144 | tf_op jit(solution)/shard_map/all_to_all | solution.py:88
  53.0 20.9 %collective-permute-start.4 = (bf16[4,64,512]{2,1,0:T(8,128)(2,1)S(1)}, bf16[4,64,512]{2,1,0:T(8,128)(2,1)S(1)}, u32[]{:S(2)}, u32[]{:S(2)}) collective-permute-start(bf16[4,64,512]{2,1,0:T(8,128)(2,1)S(1)} %all-to-all-done.refs_2_.weight0_hbm), channel_id=1, source_target_pairs={{480,0},{481,1},{482,2},{483,3},{484,4},{485,5},{486,6},{487,7},{4... | collective-permute-start | bytes 786440 | tf_op jit(solution)/shard_map/ppermute | solution.py:274
  56.3 17.6 %collective-permute-start.3 = (bf16[4,64,512]{2,1,0:T(8,128)(2,1)S(1)}, bf16[4,64,512]{2,1,0:T(8,128)(2,1)S(1)}, u32[]{:S(2)}, u32[]{:S(2)}) collective-permute-start(bf16[4,64,512]{2,1,0:T(8,128)(2,1)S(1)} %all-to-all-done.refs_2_.weight0_hbm), channel_id=1, source_target_pairs={{32,0},{33,1},{34,2},{35,3},{36,4},{37,5},{38,6},{39,7},{40,8},{41... | collective-permute-start | bytes 786440 | tf_op jit(solution)/shard_map/ppermute | solution.py:274
  61.4 10.0 %collective-permute-start.6 = (bf16[2,64,512]{2,1,0:T(8,128)(2,1)S(1)}, bf16[2,64,512]{2,1,0:T(8,128)(2,1)S(1)}, u32[]{:S(2)}, u32[]{:S(2)}) collective-permute-start(bf16[2,64,512]{2,1,0:T(8,128)(2,1)S(1)} %get-tuple-element.62), channel_id=1, source_target_pairs={{448,0},{449,1},{450,2},{451,3},{452,4},{453,5},{454,6},{455,7},{4... | collective-permute-start | bytes 393224 | tf_op jit(solution)/shard_map/ppermute | solution.py:274
  63.3 9.9 %collective-permute-start.5 = (bf16[2,64,512]{2,1,0:T(8,128)(2,1)S(1)}, bf16[2,64,512]{2,1,0:T(8,128)(2,1)S(1)}, u32[]{:S(2)}, u32[]{:S(2)}) collective-permute-start(bf16[2,64,512]{2,1,0:T(8,128)(2,1)S(1)} %get-tuple-element.63), channel_id=1, source_target_pairs={{64,0},{65,1},{66,2},{67,3},{68,4},{69,5},{70,6},{71,7},{72,8},{73... | collective-permute-start | bytes 393224 | tf_op jit(solution)/shard_map/ppermute | solution.py:274
  73.9 2.1 copy-start.5
  73.9 2.1 copy-start.7
  73.9 1.1 copy-start.11
  75.0 0.9 copy-start.14
  76.0 0.7 copy-start.19
  77.3 11.8 %collective-permute-start.7 = (bf16[4,1024,128]{2,1,0:T(8,128)(2,1)S(1)}, bf16[4,1024,128]{2,1,0:T(8,128)(2,1)S(1)}, u32[]{:S(2)}, u32[]{:S(2)}) collective-permute-start(bf16[4,1024,128]{2,1,0:T(8,128)(2,1)S(1)} %get-tuple-element.35.own_hbm), channel_id=1, source_target_pairs={{1,0},{0,1},{3,2},{2,3},{5,4},{4,5},{7,6},{6,7},{9,8},{8,9},{11,10... | collective-permute-start | bytes 3145736 | tf_op jit(solution)/shard_map/ppermute | solution.py:274
  79.2 27.9 %all-to-all-start.3 = ((bf16[4,32,128]{2,1,0:T(8,128)(2,1)}), bf16[4,32,128]{2,1,0:T(8,128)(2,1)}, u32[]{:S(2)}, u32[]{:S(2)}) async-start(bf16[4,32,128]{2,1,0:T(8,128)(2,1)} %copy-done.23), calls=%async_computation.3 | async-start | bytes 65536 | tf_op jit(solution)/shard_map/all_to_all | solution.py:97
  89.1 1.0 copy-start.3
  90.1 1.2 copy-start.4
  91.3 0.9 copy-start.6
  92.3 0.9 copy-start.8
  93.2 0.9 copy-start.12
  94.1 0.9 copy-start.15
  98.4 32.5 %collective-permute-start.8 = (f32[256,512]{1,0:T(8,128)}, f32[256,512]{1,0:T(8,128)S(1)}, u32[]{:S(2)}, u32[]{:S(2)}) collective-permute-start(f32[256,512]{1,0:T(8,128)} %get-tuple-element.38), channel_id=1, source_target_pairs={{24,0},{25,1},{26,2},{27,3},{28,4},{29,5},{30,6},{31,7},{0,8},{1,9... | collective-permute-start | bytes 1572872 | tf_op jit(solution)/shard_map/ppermute | solution.py:274
  100.9 30.1 %collective-permute-start.9 = (f32[256,512]{1,0:T(8,128)}, f32[256,512]{1,0:T(8,128)S(1)}, u32[]{:S(2)}, u32[]{:S(2)}) collective-permute-start(f32[256,512]{1,0:T(8,128)} %get-tuple-element.39), channel_id=1, source_target_pairs={{16,0},{17,1},{18,2},{19,3},{20,4},{21,5},{22,6},{23,7},{24,8},{25... | collective-permute-start | bytes 1572872 | tf_op jit(solution)/shard_map/ppermute | solution.py:274
  105.2 25.8 %collective-permute-start.10 = (f32[256,512]{1,0:T(8,128)}, f32[256,512]{1,0:T(8,128)}, u32[]{:S(2)}, u32[]{:S(2)}) collective-permute-start(f32[256,512]{1,0:T(8,128)} %get-tuple-element.40), channel_id=1, source_target_pairs={{8,0},{9,1},{10,2},{11,3},{12,4},{13,5},{14,6},{15,7},{16,8},{17,9... | collective-permute-start | bytes 1572872 | tf_op jit(solution)/shard_map/ppermute | solution.py:274
  107.1 1.0 copy-start.20
  108.8 22.1 %copy-start.2 = (bf16[256,512]{1,0:T(8,128)(2,1)S(1)}, bf16[256,512]{1,0:T(8,128)(2,1)}, u32[]{:S(2)}) copy-start(bf16[256,512]{1,0:T(8,128)(2,1)} %refs_0_.8) | copy-start | bytes 786436
  131.7 11.3 %collective-permute-start.13 = (bf16[256,512]{1,0:T(8,128)(2,1)S(1)}, bf16[256,512]{1,0:T(8,128)(2,1)S(1)}, u32[]{:S(2)}, u32[]{:S(2)}) collective-permute-start(bf16[256,512]{1,0:T(8,128)(2,1)S(1)} %get-tuple-element.41.refs_1_), channel_id=1, source_target_pairs={{24,0},{25,1},{26,2},{27,3},{28,4},{29,5},{30,6},{31,7},{0,8},{1,9... | collective-permute-start | bytes 786440 | tf_op jit(solution)/shard_map/ppermute | solution.py:274
  134.2 12.6 %collective-permute-start.12 = (bf16[256,512]{1,0:T(8,128)(2,1)S(1)}, bf16[256,512]{1,0:T(8,128)(2,1)S(1)}, u32[]{:S(2)}, u32[]{:S(2)}) collective-permute-start(bf16[256,512]{1,0:T(8,128)(2,1)S(1)} %get-tuple-element.41.refs_1_), channel_id=1, source_target_pairs={{16,0},{17,1},{18,2},{19,3},{20,4},{21,5},{22,6},{23,7},{24,8},{25... | collective-permute-start | bytes 786440 | tf_op jit(solution)/shard_map/ppermute | solution.py:274
  138.5 12.4 %collective-permute-start.11 = (bf16[256,512]{1,0:T(8,128)(2,1)S(1)}, bf16[256,512]{1,0:T(8,128)(2,1)S(1)}, u32[]{:S(2)}, u32[]{:S(2)}) collective-permute-start(bf16[256,512]{1,0:T(8,128)(2,1)S(1)} %get-tuple-element.41.refs_1_), channel_id=1, source_target_pairs={{8,0},{9,1},{10,2},{11,3},{12,4},{13,5},{14,6},{15,7},{16,8},{17,9... | collective-permute-start | bytes 786440 | tf_op jit(solution)/shard_map/ppermute | solution.py:274
  143.0 10.8 %copy-start.9 = (bf16[512,128]{1,0:T(8,128)(2,1)}, bf16[512,128]{1,0:T(8,128)(2,1)S(1)}, u32[]{:S(2)}) copy-start(bf16[512,128]{1,0:T(8,128)(2,1)S(1)} %get-tuple-element.43.refs_6_) | copy-start | bytes 393220
  143.0 10.8 %copy-start.17 = (bf16[256,512]{1,0:T(8,128)(2,1)}, bf16[256,512]{1,0:T(8,128)(2,1)S(1)}, u32[]{:S(2)}) copy-start(bf16[256,512]{1,0:T(8,128)(2,1)S(1)} %get-tuple-element.54.refs_3_) | copy-start | bytes 786436
  153.8 8.6 %collective-permute-start.14 = (bf16[4,4,256,128]{3,2,1,0:T(8,128)(2,1)}, bf16[4,4,256,128]{3,2,1,0:T(8,128)(2,1)S(1)}, u32[]{:S(2)}, u32[]{:S(2)}) collective-permute-start(bf16[4,4,256,128]{3,2,1,0:T(8,128)(2,1)} %get-tuple-element.45), channel_id=1, source_target_pairs={{1,0},{0,1},{3,2},{2,3},{5,4},{4,5},{7,6},{6,7},{9,8},{8,9},{11,10... | collective-permute-start | bytes 3145736 | tf_op jit(solution)/shard_map/ppermute | solution.py:274
  155.7 19.2 %all-to-all-start.5 = ((bf16[16,32,128]{2,1,0:T(8,128)(2,1)}), bf16[16,32,128]{2,1,0:T(8,128)(2,1)}, u32[]{:S(2)}, u32[]{:S(2)}) async-start(bf16[16,32,128]{2,1,0:T(8,128)(2,1)} %bitcast.17), calls=%async_computation.5 | async-start | bytes 262144 | tf_op jit(solution)/shard_map/all_to_all | solution.py:88
  163.4 0.7 copy-start.21
  164.1 36.4 %collective-permute-start.15 = (bf16[4,256,128]{2,1,0:T(8,128)(2,1)}, bf16[4,256,128]{2,1,0:T(8,128)(2,1)S(1)}, u32[]{:S(2)}, u32[]{:S(2)}) collective-permute-start(bf16[4,256,128]{2,1,0:T(8,128)(2,1)} %get-tuple-element.47), channel_id=1, source_target_pairs={{6,0},{7,1},{0,2},{1,3},{2,4},{3,5},{4,6},{5,7},{14,8},{15,9},{8,1... | collective-permute-start | bytes 786440 | tf_op jit(solution)/shard_map/ppermute | solution.py:274
  167.8 32.7 %collective-permute-start.16 = (bf16[4,256,128]{2,1,0:T(8,128)(2,1)}, bf16[4,256,128]{2,1,0:T(8,128)(2,1)S(1)}, u32[]{:S(2)}, u32[]{:S(2)}) collective-permute-start(bf16[4,256,128]{2,1,0:T(8,128)(2,1)} %get-tuple-element.48), channel_id=1, source_target_pairs={{4,0},{5,1},{6,2},{7,3},{0,4},{1,5},{2,6},{3,7},{12,8},{13,9},{14,... | collective-permute-start | bytes 786440 | tf_op jit(solution)/shard_map/ppermute | solution.py:274
  172.1 28.4 %collective-permute-start.17 = (bf16[4,256,128]{2,1,0:T(8,128)(2,1)}, bf16[4,256,128]{2,1,0:T(8,128)(2,1)S(1)}, u32[]{:S(2)}, u32[]{:S(2)}) collective-permute-start(bf16[4,256,128]{2,1,0:T(8,128)(2,1)} %get-tuple-element.49), channel_id=1, source_target_pairs={{2,0},{3,1},{4,2},{5,3},{6,4},{7,5},{0,6},{1,7},{10,8},{11,9},{12,... | collective-permute-start | bytes 786440 | tf_op jit(solution)/shard_map/ppermute | solution.py:274
  201.2 7.2 %copy-start.22 = (bf16[4,256,128]{2,1,0:T(8,128)(2,1)S(1)}, bf16[4,256,128]{2,1,0:T(8,128)(2,1)}, u32[]{:S(2)}) copy-start(bf16[4,256,128]{2,1,0:T(8,128)(2,1)} %copy-done.21) | copy-start | bytes 786436
  201.2 23.5 %all-to-all-start.7 = ((bf16[16,32,128]{2,1,0:T(8,128)(2,1)}), bf16[16,32,128]{2,1,0:T(8,128)(2,1)S(1)}, u32[]{:S(2)}, u32[]{:S(2)}) async-start(bf16[16,32,128]{2,1,0:T(8,128)(2,1)} %far_scan.3), calls=%async_computation.7 | async-start | bytes 262144 | tf_op jit(solution)/shard_map/all_to_all | solution.py:109
  208.4 9.4 %copy-start.18 = (bf16[256,512]{1,0:T(8,128)(2,1)S(1)}, bf16[256,512]{1,0:T(8,128)(2,1)}, u32[]{:S(2)}) copy-start(bf16[256,512]{1,0:T(8,128)(2,1)} %copy-done.17) | copy-start | bytes 786436
  209.1 10.7 %collective-permute-start.18 = (bf16[256,128]{1,0:T(8,128)(2,1)S(1)}, bf16[256,128]{1,0:T(8,128)(2,1)S(1)}, u32[]{:S(2)}, u32[]{:S(2)}) collective-permute-start(bf16[256,128]{1,0:T(8,128)(2,1)S(1)} %get-tuple-element.51), channel_id=1, source_target_pairs={{24,0},{25,1},{26,2},{27,3},{28,4},{29,5},{30,6},{31,7},{0,8},{1,9... | collective-permute-start | bytes 196616 | tf_op jit(solution)/shard_map/ppermute | solution.py:274
  211.1 8.7 %collective-permute-start.19 = (bf16[256,128]{1,0:T(8,128)(2,1)S(1)}, bf16[256,128]{1,0:T(8,128)(2,1)S(1)}, u32[]{:S(2)}, u32[]{:S(2)}) collective-permute-start(bf16[256,128]{1,0:T(8,128)(2,1)S(1)} %get-tuple-element.52), channel_id=1, source_target_pairs={{16,0},{17,1},{18,2},{19,3},{20,4},{21,5},{22,6},{23,7},{24,8},{25... | collective-permute-start | bytes 196616 | tf_op jit(solution)/shard_map/ppermute | solution.py:274
  215.9 7.4 %collective-permute-start.20 = (bf16[256,128]{1,0:T(8,128)(2,1)S(1)}, bf16[256,128]{1,0:T(8,128)(2,1)S(1)}, u32[]{:S(2)}, u32[]{:S(2)}) collective-permute-start(bf16[256,128]{1,0:T(8,128)(2,1)S(1)} %get-tuple-element.53), channel_id=1, source_target_pairs={{8,0},{9,1},{10,2},{11,3},{12,4},{13,5},{14,6},{15,7},{16,8},{17,9... | collective-permute-start | bytes 196616 | tf_op jit(solution)/shard_map/ppermute | solution.py:274
  (3 other events, 1.9 us)

commit v4 on v2

--- a/solution.py
+++ b/solution.py
@@ -1,3 +1,5 @@
+import math
+
 import jax
 import jax.numpy as jnp
 from jax import lax
@@ -6,11 +8,11 @@
 from jax.sharding import Mesh, PartitionSpec as P
 
 HEAD_DIM = 128
-NEAR = 16
 F32 = jnp.float32
 BF16 = jnp.bfloat16
-AXES = ("zh", "zl", "y", "x", "core")
-SIZES = (4, 4, 4, 4, 2)
+AXES = ("zh", "zm", "zl", "y", "x", "core")
+SIZES = (4, 2, 2, 4, 4, 2)
+SEQ = AXES[:4]
 PARAMS = pltpu.CompilerParams(vmem_limit_bytes=24 * 1024 * 1024)
 
 
@@ -70,8 +72,8 @@
         total_ref[at] = total
 
 
-def far_kernel(reverse, group_ref, scan_ref, totals_ref, out_ref):
-    group = group_ref[0]
+def far_kernel(reverse, split, place_ref, scan_ref, totals_ref, out_ref):
+    group = place_ref[1 + split]
     offset = jnp.zeros(scan_ref.shape[1:], F32)
     for other in range(totals_ref.shape[0]):
         counts = other > group if reverse else other < group
@@ -80,23 +82,24 @@
         out_ref[at] = (scan_ref[at] + offset).astype(BF16)
 
 
-def outside_sum(local, group, reverse, grads=()):
-    near = ("zl", "y")
-    piece = (NEAR, local.shape[0] // NEAR, HEAD_DIM)
+def outside_sum(local, split, reverse, place, grads=()):
+    far, near = SEQ[:split], SEQ[split:]
+    blocks = lax.axis_size(near)
+    piece = (blocks, local.shape[0] // blocks, HEAD_DIM)
     pieces = lax.all_to_all(local.reshape(piece), near, 0, 0, tiled=True)
     stacked = (shape_of((len(grads),) + grads[0].shape, BF16),) if grads else ()
     scan, total, *stack = call(
         lambda *refs: near_kernel(reverse, *refs),
-        (shape_of(piece, F32), shape_of((SIZES[0],) + piece[1:], BF16)) + stacked,
+        (shape_of(piece, F32), shape_of((lax.axis_size(far),) + piece[1:], BF16)) + stacked,
         pieces, *grads,
         name="near_scan",
     )
     stack += [permute(own, lambda across, half: (across, 1 - half)) for own in stack]
-    totals = lax.all_to_all(total, "zh", 0, 0, tiled=True)
+    totals = lax.all_to_all(total, far, 0, 0, tiled=True)
     sums = call(
-        lambda *refs: far_kernel(reverse, *refs),
+        lambda *refs: far_kernel(reverse, split, *refs),
         shape_of(piece, BF16),
-        group,
+        place,
         scan,
         totals,
         smem=1,
@@ -119,11 +122,11 @@
 
 
 def middle_kernel(
-    place_ref, own_hbm, other_hbm, weight_hbm, query_ref, numer_ref,
+    place_ref, own_ref, other_ref, weight_hbm, query_ref, numer_ref,
     numer_grad_ref, local_grad_ref, partial_hbm,
-    weight_ref, grad_ref, attended_ref, out_dir_ref, partial_ref, in_sems, grad_sems, out_sems,
+    weight_ref, attended_ref, out_dir_ref, partial_ref, in_sems, out_sems,
 ):
-    chips, rows, width = own_hbm.shape
+    chips, rows, width = own_ref.shape
     across, core = place_ref[0], place_ref[1]
 
     def share(step):
@@ -135,15 +138,8 @@
         pltpu.make_async_copy(weight_hbm.at[share(step), :], weight_ref.at[step], in_sems.at[step])
         for step in range(2 * chips)
     ]
-    grads = [
-        pltpu.make_async_copy(
-            (own_hbm if step % 2 == 0 else other_hbm).at[step // 2], grad_ref.at[step], grad_sems.at[step]
-        )
-        for step in range(2 * chips)
-    ]
-    for fetch, grad in zip(fetches, grads):
+    for fetch in fetches:
         fetch.start()
-        grad.start()
     for head in range(width // HEAD_DIM):
         cols = head_cols(head)
         numer = numer_ref[:, cols]
@@ -152,8 +148,8 @@
     sends = []
     for step in range(2 * chips):
         fetches[step].wait()
-        grads[step].wait()
-        term = dot(grad_ref[step], weight_ref[step], ((1,), (0,)))
+        grad_ref = own_ref if step % 2 == 0 else other_ref
+        term = dot(grad_ref[step // 2], weight_ref[step], ((1,), (0,)))
         if step == 0:
             out_dir_ref[...] = term
         else:
@@ -189,19 +185,17 @@
             shape_of((width, HEAD_DIM), BF16),
             shape_of((rows, shares * width), BF16),
         ),
-        in_specs=[pl.BlockSpec(memory_space=pltpu.SMEM), hbm, hbm, hbm, vmem, vmem],
+        in_specs=[pl.BlockSpec(memory_space=pltpu.SMEM), vmem, vmem, hbm, vmem, vmem],
         out_specs=[vmem, vmem, hbm],
         scratch_shapes=[
             pltpu.VMEM((shares, width, width), BF16),
-            pltpu.VMEM((shares, rows, width), BF16),
             pltpu.VMEM((rows, width), BF16),
             pltpu.VMEM((rows, width), F32),
             pltpu.VMEM((shares, rows, width), BF16),
             pltpu.SemaphoreType.DMA((shares,)),
             pltpu.SemaphoreType.DMA((shares,)),
-            pltpu.SemaphoreType.DMA((shares,)),
         ],
-        compiler_params=pltpu.CompilerParams(vmem_limit_bytes=60 * 1024 * 1024),
+        compiler_params=pltpu.CompilerParams(vmem_limit_bytes=50 * 1024 * 1024),
         name="middle",
     )(place, own, other, weight, queries, numer)
 
@@ -232,9 +226,9 @@
 
 
 def permute(value, move):
-    zh, zl, y, x, core = SIZES
+    *seqs, x, core = SIZES
     pairs = []
-    for seq in range(zh * zl * y):
+    for seq in range(math.prod(seqs)):
         for across in range(x):
             for half in range(core):
                 to_across, to_half = move(across, half)
@@ -246,26 +240,26 @@
 
 def per_device(queries, key_rows, values, out_weight, out_grad):
     rows, width = queries.shape
-    group = lax.axis_index("zh").astype(jnp.int32).reshape(1)
-    place = jnp.stack([lax.axis_index("x"), lax.axis_index("core")]).astype(jnp.int32)
+    place = [lax.axis_index(axes) for axes in ("x", "core", SEQ[:1], SEQ[:2])]
+    place = jnp.stack(place).astype(jnp.int32)
 
     weight = out_weight.T
-    copies = jnp.broadcast_to(weight[None], (SIZES[2],) + weight.shape)
+    copies = jnp.broadcast_to(weight[None], (SIZES[3],) + weight.shape)
     weight = lax.all_to_all(copies, "y", 0, 0, tiled=True).reshape(-1, width)
-    weight = lax.all_gather(weight, ("zh", "zl"), axis=0, tiled=True)
+    weight = lax.all_gather(weight, SEQ[:3], axis=0, tiled=True)
 
     grads = [out_grad] + [
         permute(out_grad, lambda across, half, ahead=ahead: (across - ahead, half)) for ahead in (1, 2, 3)
     ]
 
     local_state = call(state_kernel, shape_of((width, HEAD_DIM), BF16), key_rows, values, name="state")
-    prefix, own_grads, other_grads = outside_sum(local_state, group, False, grads)
+    prefix, own_grads, other_grads = outside_sum(local_state, 1, False, place, grads)
     numer = call(
         forward_kernel, shape_of((rows, width), F32), queries, key_rows, values, prefix, name="forward"
     )
     numer_grad, local_grad, partial_out = middle(place, own_grads, other_grads, weight, queries, numer)
     mixed = lax.psum_scatter(partial_out, ("x", "core"), scatter_dimension=1, tiled=True)
-    (suffix,) = outside_sum(local_grad, group, True)
+    (suffix,) = outside_sum(local_grad, 2, True, place)
     query_out, key_part, value_part = call(
         backward_kernel,
         (shape_of((rows, width), BF16),) + (shape_of((rows, width), F32),) * 2,
@@ -283,12 +277,12 @@
 
 def solution(mesh):
     fine = Mesh(mesh.devices.reshape(SIZES), AXES)
-    seq, head = ("zh", "zl", "y"), ("x", "core")
-    rows = P(seq, head)
+    head = AXES[4:]
+    rows = P(SEQ, head)
     return jax.shard_map(
         per_device,
         mesh=fine,
-        in_specs=(rows, rows, rows, P(head, seq), rows),
+        in_specs=(rows, rows, rows, P(head, SEQ), rows),
         out_specs=(rows, rows, rows, rows),
         check_vma=False,
     )

time: 167 us -> 164 us (0.982)
  blocking collectives: 45.4 us -> 60.9 us
  waiting for transfers between devices: 45.5 us -> 33.6 us
  starting transfers between devices: 41 us -> 34.9 us
    all_to_all x1 -> x2, blocking collectives: 19.1 us -> 38.4 us  [the longest x1 20.7 us: outside_sum(): totals = lax.all_to_all(total, far, 0, 0, tiled=True)]
    all_to_all x2 -> x1, waiting for transfers between devices: 16.7 us -> 3.63 us  [outside_sum(): lax.all_to_all(sums, near, 0, 0, tiled=True).reshape(local.shape)]
    all_to_all x2 -> x1, starting transfers between devices: 10.1 us -> 4.02 us  [outside_sum(): lax.all_to_all(sums, near, 0, 0, tiled=True).reshape(local.shape)]
    all_to_all x1, blocking collectives: 15.2 us -> 11.4 us  [outside_sum(): pieces = lax.all_to_all(local.reshape(piece), near, 0, 0, tiled=True)]
    unnamed x22 -> x18, local copies, waits for them, and re-layouts: 4.69 us -> 5.16 us
  transfers between devices with their start and end apart: 10 -> 9, of which waited for: 7 -> 6; matrix products, arithmetic and copies ran while one was open for 0% -> 0% of each run, Pallas kernels for 4% -> 4%
where the time goes in v4:
time: 164 us; the launch traced here: 163 us
  blocking collectives  60.9 us (37%)
  starting transfers between devices  34.9 us (21%)
  waiting for transfers between devices  33.6 us (20%)
  between operations  14.2 us (9%)
  Pallas kernels  13.3 us (8%)
  local copies, waits for them, and re-layouts  6.08 us (4%)
    all_to_all x1, blocking collectives, outside_sum(): totals = lax.all_to_all(total, far, 0, 0, tiled=True)  20.7 us
    all_to_all x1, blocking collectives, outside_sum(): lax.all_to_all(sums, near, 0, 0, tiled=True).reshape(local.shape)  17.8 us
    all_to_all x1, waiting for transfers between devices, outside_sum(): totals = lax.all_to_all(total, far, 0, 0, tiled=True)  13.6 us
    all_to_all x1, starting transfers between devices, outside_sum(): totals = lax.all_to_all(total, far, 0, 0, tiled=True)  12.4 us
    ppermute x4, starting transfers between devices, permute(): return lax.ppermute(value, AXES, pairs)  11.8 us
    all_to_all x1, blocking collectives, outside_sum(): pieces = lax.all_to_all(local.reshape(piece), near, 0, 0, tiled=True)  11.4 us
    all_to_all x1, blocking collectives, per_device(): weight = lax.all_to_all(copies, 'y', 0, 0, tiled=True).reshape(-1, width)  11 us
    all_gather x1, waiting for transfers between devices, per_device(): weight = lax.all_gather(weight, SEQ[:3], axis=0, tiled=True)  10.4 us
  transfers between devices with their start and end apart: 9, of which 6 were waited for; matrix products, arithmetic and copies ran while one was open for 0% of the time, Pallas kernels for 4%

profile of v4, /device:TPU:2, one launch (start us, length us, event | category | flops | bytes accessed | tf_op | source)
XLA Modules:
  0.0 163.0 jit_solution(7166144564965974961)
XLA Ops:
  7.2 0.0 copy-start.3
  7.2 0.0 copy-start.1
  7.2 0.0 copy-start.4
  7.2 0.0 all-gather.2.cloned.1.call-start
  7.2 0.9 broadcast_in_dim.2
  8.2 11.0 %all_to_all.35 = bf16[4,64,512]{2,1,0:T(8,128)(2,1)} all-to-all(bf16[4,64,512]{2,1,0:T(8,128)(2,1)S(1)} %broadcast_in_dim.2), channel_id=1, replica_groups=mesh['zh'=4,'zm'=2,'zl'=2,'y'=4,'x'=4,'core'=2] {'y'}, dimensions={0} | all-to-all | bytes 524288 | tf_op jit(solution)/shard_map/all_to_all | solution.py:248
  19.2 0.0 all-gather.2.cloned.1.call-update
  19.2 0.0 copy-start
  19.3 0.9 copy-done
  20.2 0.0 copy-start.2
  20.2 0.9 copy-done.2
  21.1 0.9 state.1
  22.1 6.6 %all-to-all-start = ((bf16[16,32,128]{2,1,0:T(8,128)(2,1)}), bf16[16,32,128]{2,1,0:T(8,128)(2,1)S(1)}, u32[]{:S(2)}, u32[]{:S(2)}) async-start(bf16[16,32,128]{2,1,0:T(8,128)(2,1)} %bitcast.4), calls=%async_computation | async-start | bytes 262144 | tf_op jit(solution)/shard_map/all_to_all | solution.py:89
  28.7 4.0 %collective-permute-start.1 = (bf16[256,512]{1,0:T(8,128)(2,1)}, bf16[256,512]{1,0:T(8,128)(2,1)S(1)}, u32[]{:S(2)}, u32[]{:S(2)}) collective-permute-start(bf16[256,512]{1,0:T(8,128)(2,1)} %refs_1_.6), channel_id=1, source_target_pairs={{0,4},{1,5},{2,6},{3,7},{4,0},{5,1},{6,2},{7,3},{8,12},{9,13},{10,... | collective-permute-start | bytes 786440 | tf_op jit(solution)/shard_map/ppermute | solution.py:238
  32.7 3.3 %collective-permute-start = (bf16[256,512]{1,0:T(8,128)(2,1)}, bf16[256,512]{1,0:T(8,128)(2,1)S(1)}, u32[]{:S(2)}, u32[]{:S(2)}) collective-permute-start(bf16[256,512]{1,0:T(8,128)(2,1)} %refs_1_.6), channel_id=1, source_target_pairs={{0,6},{1,7},{2,0},{3,1},{4,2},{5,3},{6,4},{7,5},{8,14},{9,15},{10,... | collective-permute-start | bytes 786440 | tf_op jit(solution)/shard_map/ppermute | solution.py:238
  36.1 2.5 %collective-permute-start.2 = (bf16[256,512]{1,0:T(8,128)(2,1)}, bf16[256,512]{1,0:T(8,128)(2,1)S(1)}, u32[]{:S(2)}, u32[]{:S(2)}) collective-permute-start(bf16[256,512]{1,0:T(8,128)(2,1)} %refs_1_.6), channel_id=1, source_target_pairs={{0,2},{1,3},{2,4},{3,5},{4,6},{5,7},{6,0},{7,1},{8,10},{9,11},{10,... | collective-permute-start | bytes 786440 | tf_op jit(solution)/shard_map/ppermute | solution.py:238
  38.6 2.9 %collective-permute-done.1.refs_3_ = bf16[256,512]{1,0:T(8,128)(2,1)S(1)} collective-permute-done((bf16[256,512]{1,0:T(8,128)(2,1)}, bf16[256,512]{1,0:T(8,128)(2,1)S(1)}, u32[]{:S(2)}, u32[]{:S(2)}) %collective-permute-start.1) | collective-permute-done | bytes 262176 | tf_op jit(solution)/shard_map/ppermute | solution.py:238
  41.5 2.8 %collective-permute-done.refs_2_ = bf16[256,512]{1,0:T(8,128)(2,1)S(1)} collective-permute-done((bf16[256,512]{1,0:T(8,128)(2,1)}, bf16[256,512]{1,0:T(8,128)(2,1)S(1)}, u32[]{:S(2)}, u32[]{:S(2)}) %collective-permute-start) | collective-permute-done | bytes 262176 | tf_op jit(solution)/shard_map/ppermute | solution.py:238
  44.3 0.3 collective-permute-done.2.refs_4_
  44.6 0.0 all-to-all-done.refs_0_
  44.6 1.0 copy-done.5
  45.5 0.7 near_scan.2
  46.2 1.9 %collective-permute-start.3 = (bf16[4,256,512]{2,1,0:T(8,128)(2,1)S(1)}, bf16[4,256,512]{2,1,0:T(8,128)(2,1)S(1)}, u32[]{:S(2)}, u32[]{:S(2)}) collective-permute-start(bf16[4,256,512]{2,1,0:T(8,128)(2,1)S(1)} %get-tuple-element.17.refs_3_.own_ref), channel_id=1, source_target_pairs={{0,1},{1,0},{2,3},{3,2},{4,5},{5,4},{6,7},{7,6},{8,9},{9,8},{10,11... | collective-permute-start | bytes 3145736 | tf_op jit(solution)/shard_map/ppermute | solution.py:238
  48.1 12.4 %all-to-all-start.2 = ((bf16[4,32,128]{2,1,0:T(8,128)(2,1)}), bf16[4,32,128]{2,1,0:T(8,128)(2,1)S(1)}, u32[]{:S(2)}, u32[]{:S(2)}) async-start(bf16[4,32,128]{2,1,0:T(8,128)(2,1)} %get-tuple-element.19), calls=%async_computation.2 | async-start | bytes 65536 | tf_op jit(solution)/shard_map/all_to_all | solution.py:98
  60.5 0.0 reduce-scatter.2.cloned.1.call-start
  60.5 0.1 pad_add_fusion.refs_0_.place_ref
  60.6 13.6 %all-to-all-done.2.refs_2_ = bf16[4,32,128]{2,1,0:T(8,128)(2,1)S(1)} async-done(((bf16[4,32,128]{2,1,0:T(8,128)(2,1)}), bf16[4,32,128]{2,1,0:T(8,128)(2,1)S(1)}, u32[]{:S(2)}, u32[]{:S(2)}) %all-to-all-start.2) | async-done | bytes 32800 | tf_op jit(solution)/shard_map/all_to_all | solution.py:98
  74.2 0.0 collective-permute-done.3.refs_4_.other_ref
  74.2 0.6 far_scan.2
  74.8 17.8 %all_to_all.36 = bf16[16,32,128]{2,1,0:T(8,128)(2,1)S(1)} all-to-all(bf16[16,32,128]{2,1,0:T(8,128)(2,1)S(1)} %far_scan.2), channel_id=1, replica_groups=mesh['zh'=4,'zm'=2,'zl'=2,'y'=4,'x'=4,'core'=2] {'zm','zl','y'}, dimensions={0} | all-to-all | bytes 262144 | tf_op jit(solution)/shard_map/all_to_all | solution.py:109
  92.5 0.0 copy-done.3
  92.6 0.0 copy-done.1
  92.6 0.0 copy-done.4
  92.6 0.7 forward.1.numer_ref
  93.2 10.4 %all-gather.2.cloned.1.call-done.weight_hbm = bf16[4096,512]{1,0:T(8,128)(2,1)} async-done(((bf16[256,512]{1,0:T(8,128)(2,1)}), bf16[4096,512]{1,0:T(8,128)(2,1)}) %all-gather.2.cloned.1.call-update) | async-done | bytes 4194320 | tf_op jit(solution)/shard_map/all_gather | solution.py:249
  103.6 6.1 %middle.1 = (bf16[256,512]{1,0:T(8,128)(2,1)S(1)}, bf16[512,128]{1,0:T(8,128)(2,1)S(1)}, bf16[256,4096]{1,0:T(8,128)(2,1)}) custom-call(s32[4]{0:T(128)S(1)} %pad_add_fusion.refs_0_.place_ref, bf16[4,256,512]{2,1,0:T(8,128)(2,1)S(1)} %get-tuple-element.17.refs_3_.own_ref, bf16[4,256,512]{2,1,0:T(8,128)(2,1)S(1)} %collective-permute-done.3.refs_4_.other_ref, ...), custom_call_target="tpu_custom_call" | custom-call | tf_op jit(solution)/shard_map/middle/pallas_call | solution.py:181
  109.7 0.0 copy-start.6
  109.7 0.7 copy-done.6
  110.4 0.7 copy-done.8
  111.1 0.0 reduce-scatter.2.cloned.1.call-update
  111.1 11.4 %all_to_all.37.refs_0_ = bf16[8,64,128]{2,1,0:T(8,128)(2,1)S(1)} all-to-all(bf16[8,64,128]{2,1,0:T(8,128)(2,1)} %bitcast.13), channel_id=1, replica_groups=mesh['zh'=4,'zm'=2,'zl'=2,'y'=4,'x'=4,'core'=2] {'zl','y'}, dimensions={0} | all-to-all | bytes 262144 | tf_op jit(solution)/shard_map/all_to_all | solution.py:89
  122.5 20.7 %all_to_all.38.refs_2_ = bf16[8,64,128]{2,1,0:T(8,128)(2,1)S(1)} all-to-all(bf16[8,64,128]{2,1,0:T(8,128)(2,1)S(1)} %get-tuple-element.25), channel_id=1, replica_groups=mesh['zh'=4,'zm'=2,'zl'=2,'y'=4,'x'=4,'core'=2] {'zh','zm'}, dimensions={0} | all-to-all | bytes 262144 | tf_op jit(solution)/shard_map/all_to_all | solution.py:98
  143.2 1.2 far_scan.3
  144.4 4.0 %all-to-all-start.6 = ((bf16[8,64,128]{2,1,0:T(8,128)(2,1)}), bf16[8,64,128]{2,1,0:T(8,128)(2,1)S(1)}, u32[]{:S(2)}, u32[]{:S(2)}) async-start(bf16[8,64,128]{2,1,0:T(8,128)(2,1)} %far_scan.3), calls=%async_computation.7 | async-start | bytes 262144 | tf_op jit(solution)/shard_map/all_to_all | solution.py:109
  148.5 0.9 copy-done.7
  149.4 2.0 %backward.1 = (bf16[256,512]{1,0:T(8,128)(2,1)}, f32[256,512]{1,0:T(8,128)S(1)}, f32[256,512]{1,0:T(8,128)S(1)}) custom-call(bf16[256,512]{1,0:T(8,128)(2,1)S(1)} %copy-done.4, bf16[256,512]{1,0:T(8,128)(2,1)S(1)} %copy-done.1, bf16[256,512]{1,0:T(8,128)(2,1)S(1)} %copy-done.3, bf16[256,512]{1,0:T(8,128)(2,1)S(1)} %copy-done.7, bf16[512,128]{1,0:T(8,128)(2,1)S(1)} %bitcast.11), custom_call_target="tpu_custom_call" | custom-call | tf_op jit(solution)/shard_map/backward/pallas_call | solution.py:35
  151.4 3.6 %all-to-all-done.6 = bf16[8,64,128]{2,1,0:T(8,128)(2,1)S(1)} async-done(((bf16[8,64,128]{2,1,0:T(8,128)(2,1)}), bf16[8,64,128]{2,1,0:T(8,128)(2,1)S(1)}, u32[]{:S(2)}, u32[]{:S(2)}) %all-to-all-start.6) | async-done | bytes 131104 | tf_op jit(solution)/shard_map/all_to_all | solution.py:109
  155.0 1.1 suffix.1
  (5 shorter events, 0.0 us)
Async XLA Ops:
  7.2 85.4 %copy-start.3 = (bf16[256,512]{1,0:T(8,128)(2,1)S(1)}, bf16[256,512]{1,0:T(8,128)(2,1)}, u32[]{:S(2)}) copy-start(bf16[256,512]{1,0:T(8,128)(2,1)} %refs_1_.9) | copy-start | bytes 786436
  7.2 85.4 %copy-start.1 = (bf16[256,512]{1,0:T(8,128)(2,1)S(1)}, bf16[256,512]{1,0:T(8,128)(2,1)}, u32[]{:S(2)}) copy-start(bf16[256,512]{1,0:T(8,128)(2,1)} %refs_0_.7) | copy-start | bytes 786436
  7.2 85.4 %copy-start.4 = (bf16[256,512]{1,0:T(8,128)(2,1)S(1)}, bf16[256,512]{1,0:T(8,128)(2,1)}, u32[]{:S(2)}) copy-start(bf16[256,512]{1,0:T(8,128)(2,1)} %refs_0_.6) | copy-start | bytes 786436
  7.2 96.4 %all-gather.2.cloned.1.call-start = ((), (), s32[]{:S(2)}) async-start(), calls=%async_computation.8 | async-start | bytes 4456448 | tf_op jit(solution)/shard_map/all_gather | solution.py:249
  19.2 1.0 copy-start
  20.2 0.9 copy-start.2
  22.1 22.5 %all-to-all-start = ((bf16[16,32,128]{2,1,0:T(8,128)(2,1)}), bf16[16,32,128]{2,1,0:T(8,128)(2,1)S(1)}, u32[]{:S(2)}, u32[]{:S(2)}) async-start(bf16[16,32,128]{2,1,0:T(8,128)(2,1)} %bitcast.4), calls=%async_computation | async-start | bytes 262144 | tf_op jit(solution)/shard_map/all_to_all | solution.py:89
  28.7 12.8 %collective-permute-start.1 = (bf16[256,512]{1,0:T(8,128)(2,1)}, bf16[256,512]{1,0:T(8,128)(2,1)S(1)}, u32[]{:S(2)}, u32[]{:S(2)}) collective-permute-start(bf16[256,512]{1,0:T(8,128)(2,1)} %refs_1_.6), channel_id=1, source_target_pairs={{0,4},{1,5},{2,6},{3,7},{4,0},{5,1},{6,2},{7,3},{8,12},{9,13},{10,... | collective-permute-start | bytes 786440 | tf_op jit(solution)/shard_map/ppermute | solution.py:238
  32.7 11.5 %collective-permute-start = (bf16[256,512]{1,0:T(8,128)(2,1)}, bf16[256,512]{1,0:T(8,128)(2,1)S(1)}, u32[]{:S(2)}, u32[]{:S(2)}) collective-permute-start(bf16[256,512]{1,0:T(8,128)(2,1)} %refs_1_.6), channel_id=1, source_target_pairs={{0,6},{1,7},{2,0},{3,1},{4,2},{5,3},{6,4},{7,5},{8,14},{9,15},{10,... | collective-permute-start | bytes 786440 | tf_op jit(solution)/shard_map/ppermute | solution.py:238
  36.1 8.5 %collective-permute-start.2 = (bf16[256,512]{1,0:T(8,128)(2,1)}, bf16[256,512]{1,0:T(8,128)(2,1)S(1)}, u32[]{:S(2)}, u32[]{:S(2)}) collective-permute-start(bf16[256,512]{1,0:T(8,128)(2,1)} %refs_1_.6), channel_id=1, source_target_pairs={{0,2},{1,3},{2,4},{3,5},{4,6},{5,7},{6,0},{7,1},{8,10},{9,11},{10,... | collective-permute-start | bytes 786440 | tf_op jit(solution)/shard_map/ppermute | solution.py:238
  44.6 1.0 copy-start.5
  46.2 28.0 %collective-permute-start.3 = (bf16[4,256,512]{2,1,0:T(8,128)(2,1)S(1)}, bf16[4,256,512]{2,1,0:T(8,128)(2,1)S(1)}, u32[]{:S(2)}, u32[]{:S(2)}) collective-permute-start(bf16[4,256,512]{2,1,0:T(8,128)(2,1)S(1)} %get-tuple-element.17.refs_3_.own_ref), channel_id=1, source_target_pairs={{0,1},{1,0},{2,3},{3,2},{4,5},{5,4},{6,7},{7,6},{8,9},{9,8},{10,11... | collective-permute-start | bytes 3145736 | tf_op jit(solution)/shard_map/ppermute | solution.py:238
  48.1 26.1 %all-to-all-start.2 = ((bf16[4,32,128]{2,1,0:T(8,128)(2,1)}), bf16[4,32,128]{2,1,0:T(8,128)(2,1)S(1)}, u32[]{:S(2)}, u32[]{:S(2)}) async-start(bf16[4,32,128]{2,1,0:T(8,128)(2,1)} %get-tuple-element.19), calls=%async_computation.2 | async-start | bytes 65536 | tf_op jit(solution)/shard_map/all_to_all | solution.py:98
  60.5 95.6 %reduce-scatter.2.cloned.1.call-start = ((), (), s32[]{:S(2)}) async-start(), calls=%async_computation.9 | async-start | bytes 2359296 | tf_op jit(solution)/shard_map/reduce_scatter | solution.py:261
  109.7 0.7 copy-start.6
  110.4 0.7 copy-start.8
  144.4 10.6 %all-to-all-start.6 = ((bf16[8,64,128]{2,1,0:T(8,128)(2,1)}), bf16[8,64,128]{2,1,0:T(8,128)(2,1)S(1)}, u32[]{:S(2)}, u32[]{:S(2)}) async-start(bf16[8,64,128]{2,1,0:T(8,128)(2,1)} %far_scan.3), calls=%async_computation.7 | async-start | bytes 262144 | tf_op jit(solution)/shard_map/all_to_all | solution.py:109
  148.5 0.9 copy-start.7
Sparse Core Ops, SparseCore 0:
  19.4 84.2 all-gather.1
  111.2 33.6 reduce-scatter.1

commit v5 on v4

--- a/solution.py
+++ b/solution.py
@@ -82,7 +82,7 @@
         out_ref[at] = (scan_ref[at] + offset).astype(BF16)
 
 
-def outside_sum(local, split, reverse, place, grads=()):
+def outside_sum(local, split, reverse, place, grads=(), before_far=()):
     far, near = SEQ[:split], SEQ[split:]
     blocks = lax.axis_size(near)
     piece = (blocks, local.shape[0] // blocks, HEAD_DIM)
@@ -103,7 +103,7 @@
         scan,
         totals,
         smem=1,
-        after=stack,
+        after=(*stack, *before_far),
         name="far_scan",
     )
     return lax.all_to_all(sums, near, 0, 0, tiled=True).reshape(local.shape), *stack
@@ -259,13 +259,13 @@
     )
     numer_grad, local_grad, partial_out = middle(place, own_grads, other_grads, weight, queries, numer)
     mixed = lax.psum_scatter(partial_out, ("x", "core"), scatter_dimension=1, tiled=True)
-    (suffix,) = outside_sum(local_grad, 2, True, place)
     query_out, key_part, value_part = call(
         backward_kernel,
         (shape_of((rows, width), BF16),) + (shape_of((rows, width), F32),) * 2,
         queries, key_rows, values, numer_grad, prefix,
         name="backward",
     )
+    (suffix,) = outside_sum(local_grad, 2, True, place, before_far=(query_out,))
     key_out, value_out = call(
         suffix_kernel,
         (shape_of((rows, width), BF16),) * 2,

time: 164 us -> 165 us (level)
  blocking collectives: 60.9 us -> 50.9 us
  waiting for transfers between devices: 33.6 us -> 41.1 us
  starting transfers between devices: 34.9 us -> 37.2 us
    all_to_all x1 -> x0, blocking collectives: 20.7 us -> none  [outside_sum(): totals = lax.all_to_all(total, far, 0, 0, tiled=True)]
    all_to_all x1 -> x2, waiting for transfers between devices: 13.6 us -> 24.7 us  [outside_sum(): totals = lax.all_to_all(total, far, 0, 0, tiled=True)]
    all_to_all x1 -> x2, blocking collectives: 17.8 us -> 28.3 us  [outside_sum(): lax.all_to_all(sums, near, 0, 0, tiled=True).reshape(local.shape)]
    all_to_all x1 -> x2, starting transfers between devices: 12.4 us -> 18.8 us  [outside_sum(): totals = lax.all_to_all(total, far, 0, 0, tiled=True)]
    all_to_all x1 -> x0, starting transfers between devices: 4.02 us -> none  [outside_sum(): lax.all_to_all(sums, near, 0, 0, tiled=True).reshape(local.shape)]
    all_to_all x1 -> x0, waiting for transfers between devices: 3.63 us -> none  [outside_sum(): lax.all_to_all(sums, near, 0, 0, tiled=True).reshape(local.shape)]
    unnamed x18 -> x20, local copies, waits for them, and re-layouts: 5.16 us -> 6.12 us
where the time goes in v5:
time: 165 us; the launch traced here: 164 us
  blocking collectives  50.9 us (31%)
  waiting for transfers between devices  41.1 us (25%)
  starting transfers between devices  37.2 us (23%)
  between operations  14.2 us (9%)
  Pallas kernels  13.3 us (8%)
  local copies, waits for them, and re-layouts  7.04 us (4%)
    all_to_all x2, blocking collectives, outside_sum(): lax.all_to_all(sums, near, 0, 0, tiled=True).reshape(local.shape)  28.3 us
    all_to_all x2, waiting for transfers between devices, outside_sum(): totals = lax.all_to_all(total, far, 0, 0, tiled=True)  24.7 us
    all_to_all x2, starting transfers between devices, outside_sum(): totals = lax.all_to_all(total, far, 0, 0, tiled=True)  18.8 us
    ppermute x4, starting transfers between devices, permute(): return lax.ppermute(value, AXES, pairs)  11.8 us
    all_to_all x1, blocking collectives, outside_sum(): pieces = lax.all_to_all(local.reshape(piece), near, 0, 0, tiled=True)  11.6 us
    all_to_all x1, blocking collectives, per_device(): weight = lax.all_to_all(copies, 'y', 0, 0, tiled=True).reshape(-1, width)  11 us
    all_gather x1, waiting for transfers between devices, per_device(): weight = lax.all_gather(weight, SEQ[:3], axis=0, tiled=True)  10.4 us
    pallas_call x8, Pallas kernels, call(): pl.pallas_call(body, out_shape=out_shape, in_specs=[pl.BlockSpec(memory_s...  7.21 us
  transfers between devices with their start and end apart: 9, of which 6 were waited for; matrix products, arithmetic and copies ran while one was open for 0% of the time, Pallas kernels for 4%

profile of v5, /device:TPU:2, one launch (start us, length us, event | category | flops | bytes accessed | tf_op | source)
XLA Modules:
  0.0 163.7 jit_solution(2838928791015610080)
XLA Ops:
  7.2 0.0 copy-start.3
  7.2 0.0 copy-start.1
  7.2 0.0 copy-start.4
  7.2 0.0 all-gather.2.cloned.1.call-start
  7.2 0.9 broadcast_in_dim.2
  8.2 11.0 %all_to_all.35 = bf16[4,64,512]{2,1,0:T(8,128)(2,1)} all-to-all(bf16[4,64,512]{2,1,0:T(8,128)(2,1)S(1)} %broadcast_in_dim.2), channel_id=1, replica_groups=mesh['zh'=4,'zm'=2,'zl'=2,'y'=4,'x'=4,'core'=2] {'y'}, dimensions={0} | all-to-all | bytes 524288 | tf_op jit(solution)/shard_map/all_to_all | solution.py:248
  19.2 0.0 all-gather.2.cloned.1.call-update
  19.2 0.0 copy-start
  19.3 0.9 copy-done
  20.2 0.9 copy-done.2
  21.1 0.9 state.1
  22.1 6.6 %all-to-all-start = ((bf16[16,32,128]{2,1,0:T(8,128)(2,1)}), bf16[16,32,128]{2,1,0:T(8,128)(2,1)S(1)}, u32[]{:S(2)}, u32[]{:S(2)}) async-start(bf16[16,32,128]{2,1,0:T(8,128)(2,1)} %bitcast.4), calls=%async_computation | async-start | bytes 262144 | tf_op jit(solution)/shard_map/all_to_all | solution.py:89
  28.7 4.0 %collective-permute-start.1 = (bf16[256,512]{1,0:T(8,128)(2,1)}, bf16[256,512]{1,0:T(8,128)(2,1)S(1)}, u32[]{:S(2)}, u32[]{:S(2)}) collective-permute-start(bf16[256,512]{1,0:T(8,128)(2,1)} %refs_1_.6), channel_id=1, source_target_pairs={{0,4},{1,5},{2,6},{3,7},{4,0},{5,1},{6,2},{7,3},{8,12},{9,13},{10,... | collective-permute-start | bytes 786440 | tf_op jit(solution)/shard_map/ppermute | solution.py:238
  32.7 3.3 %collective-permute-start = (bf16[256,512]{1,0:T(8,128)(2,1)}, bf16[256,512]{1,0:T(8,128)(2,1)S(1)}, u32[]{:S(2)}, u32[]{:S(2)}) collective-permute-start(bf16[256,512]{1,0:T(8,128)(2,1)} %refs_1_.6), channel_id=1, source_target_pairs={{0,6},{1,7},{2,0},{3,1},{4,2},{5,3},{6,4},{7,5},{8,14},{9,15},{10,... | collective-permute-start | bytes 786440 | tf_op jit(solution)/shard_map/ppermute | solution.py:238
  36.1 2.5 %collective-permute-start.2 = (bf16[256,512]{1,0:T(8,128)(2,1)}, bf16[256,512]{1,0:T(8,128)(2,1)S(1)}, u32[]{:S(2)}, u32[]{:S(2)}) collective-permute-start(bf16[256,512]{1,0:T(8,128)(2,1)} %refs_1_.6), channel_id=1, source_target_pairs={{0,2},{1,3},{2,4},{3,5},{4,6},{5,7},{6,0},{7,1},{8,10},{9,11},{10,... | collective-permute-start | bytes 786440 | tf_op jit(solution)/shard_map/ppermute | solution.py:238
  38.6 2.9 %collective-permute-done.1.refs_3_ = bf16[256,512]{1,0:T(8,128)(2,1)S(1)} collective-permute-done((bf16[256,512]{1,0:T(8,128)(2,1)}, bf16[256,512]{1,0:T(8,128)(2,1)S(1)}, u32[]{:S(2)}, u32[]{:S(2)}) %collective-permute-start.1) | collective-permute-done | bytes 262176 | tf_op jit(solution)/shard_map/ppermute | solution.py:238
  41.5 2.8 %collective-permute-done.refs_2_ = bf16[256,512]{1,0:T(8,128)(2,1)S(1)} collective-permute-done((bf16[256,512]{1,0:T(8,128)(2,1)}, bf16[256,512]{1,0:T(8,128)(2,1)S(1)}, u32[]{:S(2)}, u32[]{:S(2)}) %collective-permute-start) | collective-permute-done | bytes 262176 | tf_op jit(solution)/shard_map/ppermute | solution.py:238
  44.3 0.3 collective-permute-done.2.refs_4_
  44.6 0.0 all-to-all-done.refs_0_
  44.6 1.0 copy-done.5
  45.5 0.7 near_scan.2
  46.2 1.9 %collective-permute-start.3 = (bf16[4,256,512]{2,1,0:T(8,128)(2,1)S(1)}, bf16[4,256,512]{2,1,0:T(8,128)(2,1)S(1)}, u32[]{:S(2)}, u32[]{:S(2)}) collective-permute-start(bf16[4,256,512]{2,1,0:T(8,128)(2,1)S(1)} %get-tuple-element.17.refs_3_.own_ref), channel_id=1, source_target_pairs={{0,1},{1,0},{2,3},{3,2},{4,5},{5,4},{6,7},{7,6},{8,9},{9,8},{10,11... | collective-permute-start | bytes 3145736 | tf_op jit(solution)/shard_map/ppermute | solution.py:238
  48.1 12.4 %all-to-all-start.2 = ((bf16[4,32,128]{2,1,0:T(8,128)(2,1)}), bf16[4,32,128]{2,1,0:T(8,128)(2,1)S(1)}, u32[]{:S(2)}, u32[]{:S(2)}) async-start(bf16[4,32,128]{2,1,0:T(8,128)(2,1)} %get-tuple-element.19), calls=%async_computation.2 | async-start | bytes 65536 | tf_op jit(solution)/shard_map/all_to_all | solution.py:98
  60.5 0.0 reduce-scatter.2.cloned.1.call-start
  60.5 0.1 pad_add_fusion.refs_0_.place_ref
  60.6 13.6 %all-to-all-done.2.refs_2_ = bf16[4,32,128]{2,1,0:T(8,128)(2,1)S(1)} async-done(((bf16[4,32,128]{2,1,0:T(8,128)(2,1)}), bf16[4,32,128]{2,1,0:T(8,128)(2,1)S(1)}, u32[]{:S(2)}, u32[]{:S(2)}) %all-to-all-start.2) | async-done | bytes 32800 | tf_op jit(solution)/shard_map/all_to_all | solution.py:98
  74.2 0.0 collective-permute-done.3.refs_4_.other_ref
  74.2 0.6 far_scan.2
  74.8 17.8 %all_to_all.36 = bf16[16,32,128]{2,1,0:T(8,128)(2,1)S(1)} all-to-all(bf16[16,32,128]{2,1,0:T(8,128)(2,1)S(1)} %far_scan.2), channel_id=1, replica_groups=mesh['zh'=4,'zm'=2,'zl'=2,'y'=4,'x'=4,'core'=2] {'zm','zl','y'}, dimensions={0} | all-to-all | bytes 262144 | tf_op jit(solution)/shard_map/all_to_all | solution.py:109
  92.5 0.0 copy-done.3
  92.6 0.0 copy-done.1
  92.6 0.7 forward.1.numer_ref
  93.2 10.4 %all-gather.2.cloned.1.call-done.weight_hbm = bf16[4096,512]{1,0:T(8,128)(2,1)} async-done(((bf16[256,512]{1,0:T(8,128)(2,1)}), bf16[4096,512]{1,0:T(8,128)(2,1)}) %all-gather.2.cloned.1.call-update) | async-done | bytes 4194320 | tf_op jit(solution)/shard_map/all_gather | solution.py:249
  103.6 6.1 %middle.1 = (bf16[256,512]{1,0:T(8,128)(2,1)S(1)}, bf16[512,128]{1,0:T(8,128)(2,1)S(1)}, bf16[256,4096]{1,0:T(8,128)(2,1)}) custom-call(s32[4]{0:T(128)S(1)} %pad_add_fusion.refs_0_.place_ref, bf16[4,256,512]{2,1,0:T(8,128)(2,1)S(1)} %get-tuple-element.17.refs_3_.own_ref, bf16[4,256,512]{2,1,0:T(8,128)(2,1)S(1)} %collective-permute-done.3.refs_4_.other_ref, ...), custom_call_target="tpu_custom_call" | custom-call | tf_op jit(solution)/shard_map/middle/pallas_call | solution.py:181
  109.7 0.0 copy-start.7
  109.7 0.7 copy-done.7
  110.4 0.7 copy-done.9
  111.1 0.0 reduce-scatter.2.cloned.1.call-update
  111.1 11.6 %all_to_all.37.refs_0_ = bf16[8,64,128]{2,1,0:T(8,128)(2,1)S(1)} all-to-all(bf16[8,64,128]{2,1,0:T(8,128)(2,1)} %bitcast.13), channel_id=1, replica_groups=mesh['zh'=4,'zm'=2,'zl'=2,'y'=4,'x'=4,'core'=2] {'zl','y'}, dimensions={0} | all-to-all | bytes 262144 | tf_op jit(solution)/shard_map/all_to_all | solution.py:89
  122.7 0.7 near_scan.3
  123.3 6.4 %all-to-all-start.5 = ((bf16[8,64,128]{2,1,0:T(8,128)(2,1)}), bf16[8,64,128]{2,1,0:T(8,128)(2,1)S(1)}, u32[]{:S(2)}, u32[]{:S(2)}) async-start(bf16[8,64,128]{2,1,0:T(8,128)(2,1)} %get-tuple-element.25), calls=%async_computation.6 | async-start | bytes 262144 | tf_op jit(solution)/shard_map/all_to_all | solution.py:98
  129.7 0.9 copy-done.8
  130.7 2.0 %backward.1 = (bf16[256,512]{1,0:T(8,128)(2,1)}, f32[256,512]{1,0:T(8,128)S(1)}, f32[256,512]{1,0:T(8,128)S(1)}) custom-call(bf16[256,512]{1,0:T(8,128)(2,1)S(1)} %copy-done.4, bf16[256,512]{1,0:T(8,128)(2,1)S(1)} %copy-done.1, bf16[256,512]{1,0:T(8,128)(2,1)S(1)} %copy-done.3, bf16[256,512]{1,0:T(8,128)(2,1)S(1)} %copy-done.8, bf16[512,128]{1,0:T(8,128)(2,1)S(1)} %bitcast.11), custom_call_target="tpu_custom_call" | custom-call | tf_op jit(solution)/shard_map/backward/pallas_call | solution.py:35
  132.7 11.1 %all-to-all-done.5.refs_2_ = bf16[8,64,128]{2,1,0:T(8,128)(2,1)S(1)} async-done(((bf16[8,64,128]{2,1,0:T(8,128)(2,1)}), bf16[8,64,128]{2,1,0:T(8,128)(2,1)S(1)}, u32[]{:S(2)}, u32[]{:S(2)}) %all-to-all-start.5) | async-done | bytes 131104 | tf_op jit(solution)/shard_map/all_to_all | solution.py:98
  143.8 1.0 copy-done.6
  144.7 0.6 far_scan.3
  145.3 10.5 %all_to_all.38 = bf16[8,64,128]{2,1,0:T(8,128)(2,1)S(1)} all-to-all(bf16[8,64,128]{2,1,0:T(8,128)(2,1)S(1)} %far_scan.3), channel_id=1, replica_groups=mesh['zh'=4,'zm'=2,'zl'=2,'y'=4,'x'=4,'core'=2] {'zl','y'}, dimensions={0} | all-to-all | bytes 262144 | tf_op jit(solution)/shard_map/all_to_all | solution.py:109
  155.8 1.1 suffix.1
  (7 shorter events, 0.0 us)
Async XLA Ops:
  7.2 85.4 %copy-start.3 = (bf16[256,512]{1,0:T(8,128)(2,1)S(1)}, bf16[256,512]{1,0:T(8,128)(2,1)}, u32[]{:S(2)}) copy-start(bf16[256,512]{1,0:T(8,128)(2,1)} %refs_1_.9) | copy-start | bytes 786436
  7.2 85.4 %copy-start.1 = (bf16[256,512]{1,0:T(8,128)(2,1)S(1)}, bf16[256,512]{1,0:T(8,128)(2,1)}, u32[]{:S(2)}) copy-start(bf16[256,512]{1,0:T(8,128)(2,1)} %refs_0_.7) | copy-start | bytes 786436
  7.2 85.4 %copy-start.4 = (bf16[256,512]{1,0:T(8,128)(2,1)S(1)}, bf16[256,512]{1,0:T(8,128)(2,1)}, u32[]{:S(2)}) copy-start(bf16[256,512]{1,0:T(8,128)(2,1)} %refs_0_.6) | copy-start | bytes 786436
  7.2 96.4 %all-gather.2.cloned.1.call-start = ((), (), s32[]{:S(2)}) async-start(), calls=%async_computation.8 | async-start | bytes 4456448 | tf_op jit(solution)/shard_map/all_gather | solution.py:249
  19.2 1.0 copy-start
  20.2 0.9 copy-start.2
  22.1 22.5 %all-to-all-start = ((bf16[16,32,128]{2,1,0:T(8,128)(2,1)}), bf16[16,32,128]{2,1,0:T(8,128)(2,1)S(1)}, u32[]{:S(2)}, u32[]{:S(2)}) async-start(bf16[16,32,128]{2,1,0:T(8,128)(2,1)} %bitcast.4), calls=%async_computation | async-start | bytes 262144 | tf_op jit(solution)/shard_map/all_to_all | solution.py:89
  28.7 12.8 %collective-permute-start.1 = (bf16[256,512]{1,0:T(8,128)(2,1)}, bf16[256,512]{1,0:T(8,128)(2,1)S(1)}, u32[]{:S(2)}, u32[]{:S(2)}) collective-permute-start(bf16[256,512]{1,0:T(8,128)(2,1)} %refs_1_.6), channel_id=1, source_target_pairs={{0,4},{1,5},{2,6},{3,7},{4,0},{5,1},{6,2},{7,3},{8,12},{9,13},{10,... | collective-permute-start | bytes 786440 | tf_op jit(solution)/shard_map/ppermute | solution.py:238
  32.7 11.5 %collective-permute-start = (bf16[256,512]{1,0:T(8,128)(2,1)}, bf16[256,512]{1,0:T(8,128)(2,1)S(1)}, u32[]{:S(2)}, u32[]{:S(2)}) collective-permute-start(bf16[256,512]{1,0:T(8,128)(2,1)} %refs_1_.6), channel_id=1, source_target_pairs={{0,6},{1,7},{2,0},{3,1},{4,2},{5,3},{6,4},{7,5},{8,14},{9,15},{10,... | collective-permute-start | bytes 786440 | tf_op jit(solution)/shard_map/ppermute | solution.py:238
  36.1 8.5 %collective-permute-start.2 = (bf16[256,512]{1,0:T(8,128)(2,1)}, bf16[256,512]{1,0:T(8,128)(2,1)S(1)}, u32[]{:S(2)}, u32[]{:S(2)}) collective-permute-start(bf16[256,512]{1,0:T(8,128)(2,1)} %refs_1_.6), channel_id=1, source_target_pairs={{0,2},{1,3},{2,4},{3,5},{4,6},{5,7},{6,0},{7,1},{8,10},{9,11},{10,... | collective-permute-start | bytes 786440 | tf_op jit(solution)/shard_map/ppermute | solution.py:238
  44.6 1.0 copy-start.5
  46.2 28.0 %collective-permute-start.3 = (bf16[4,256,512]{2,1,0:T(8,128)(2,1)S(1)}, bf16[4,256,512]{2,1,0:T(8,128)(2,1)S(1)}, u32[]{:S(2)}, u32[]{:S(2)}) collective-permute-start(bf16[4,256,512]{2,1,0:T(8,128)(2,1)S(1)} %get-tuple-element.17.refs_3_.own_ref), channel_id=1, source_target_pairs={{0,1},{1,0},{2,3},{3,2},{4,5},{5,4},{6,7},{7,6},{8,9},{9,8},{10,11... | collective-permute-start | bytes 3145736 | tf_op jit(solution)/shard_map/ppermute | solution.py:238
  48.1 26.1 %all-to-all-start.2 = ((bf16[4,32,128]{2,1,0:T(8,128)(2,1)}), bf16[4,32,128]{2,1,0:T(8,128)(2,1)S(1)}, u32[]{:S(2)}, u32[]{:S(2)}) async-start(bf16[4,32,128]{2,1,0:T(8,128)(2,1)} %get-tuple-element.19), calls=%async_computation.2 | async-start | bytes 65536 | tf_op jit(solution)/shard_map/all_to_all | solution.py:98
  60.5 96.4 %reduce-scatter.2.cloned.1.call-start = ((), (), s32[]{:S(2)}) async-start(), calls=%async_computation.9 | async-start | bytes 2359296 | tf_op jit(solution)/shard_map/reduce_scatter | solution.py:261
  109.7 0.7 copy-start.7
  110.4 0.7 copy-start.9
  123.3 20.4 %all-to-all-start.5 = ((bf16[8,64,128]{2,1,0:T(8,128)(2,1)}), bf16[8,64,128]{2,1,0:T(8,128)(2,1)S(1)}, u32[]{:S(2)}, u32[]{:S(2)}) async-start(bf16[8,64,128]{2,1,0:T(8,128)(2,1)} %get-tuple-element.25), calls=%async_computation.6 | async-start | bytes 262144 | tf_op jit(solution)/shard_map/all_to_all | solution.py:98
  129.7 1.0 copy-start.8
  143.8 1.0 copy-start.6
Sparse Core Ops, SparseCore 0:
  19.4 84.2 all-gather.1
  111.2 33.6 reduce-scatter.1
